TPU v7x, 32 devices: a whole 2x2x4 slice. The times are simulated.
32 devices in a mesh: leaf: 32 (over z, y, x, core).
Axes of the slice: x: 2, y: 2, z: 4, core: 2. Of those that a mesh axis runs over, the one named last changes fastest.
Arguments:
- vectors: bfloat16 [64, 262144], P(None, 'leaf'), may hold values from -6 to 6
- leaf_basis: bfloat16 [64, 262144], P(None, 'leaf'), may hold values from -0.375 to 0.375
- local_transfer: bfloat16 [2016, 64, 64], P('leaf'), may hold values from -0.625 to 0.625
- near_tiles: bfloat16 [3072, 256, 256], P('leaf'), may hold values from -0.375 to 0.375
- near_rows: int32 [3072], P('leaf'), may hold values from 0 to 31, as said below
- near_cols: int32 [3072], P('leaf'), may hold values from 0 to 63, as said below
- far_tiles: bfloat16 [4608, 64, 64], P('leaf'), may hold values from -0.75 to 0.75
- far_rows: int32 [4608], P('leaf'), may hold values from 0 to 62, as said below
- far_cols: int32 [4608], P('leaf'), may hold values from 0 to 62, as said below
- far_counts: int32 [32, 9], P('leaf'), may hold values from 0 to 16, as said below
- top_transfer: float32 [30, 64, 64], replicated, may hold values from -0.625 to 0.625
- top_couple: float32 [31, 64, 64], replicated, may hold values from -0.75 to 0.75
Outputs:
- product: float32 [64, 262144], P(None, 'leaf')
Inputs may be any that keep to these rules, and one draw needn't show every extreme that they name: `near_rows`: a leaf of the tile's own device, by its index there. `near_cols`: at least near_rows and at most near_rows + 32; a value v of 32 or more names leaf v - 32 of the next device, and never occurs on the last device. `far_rows`: a local node id on the owner; a slot's two nodes are on the same level, and differ on a device's slots with itself. `far_cols`: a local node id on the peer. `far_counts`: 0 exactly where the owner plus the offset passes the last device, else at least 1; column 0 is 16.
All inputs are finite; a program needn't handle non-finite values.
Results may differ from a plain program's by a relative error of at most 0.0075.
Values may be sent and summed in bfloat16 or wider, within the bound.
A program may use at most 192 MiB of HBM per device.

v0:
```python
import jax
import jax.numpy as jnp
from jax import lax
from jax.sharding import PartitionSpec as P

highest = lax.Precision.HIGHEST


def from_behind(value, axis, steps):
    count = lax.axis_size(axis)
    initial, last = (max(0, -steps), min(count, count - steps))
    return lax.ppermute(value, axis, [(source, source + steps) for source in range(initial, last)])


def from_partner(value, axis, distance):
    mask = 2**distance
    pairs = [(source, source ^ mask) for source in range(lax.axis_size(axis))]
    return lax.ppermute(value, axis, pairs)


def pick_tile(table, position):
    return lax.dynamic_index_in_dim(table, position, 0, keepdims=False)


def body(
    vectors,
    leaf_basis,
    local_transfer,
    near_tiles,
    near_rows,
    near_cols,
    far_tiles,
    far_rows,
    far_cols,
    far_counts,
    top_transfer,
    top_couple,
):
    vec_count, points = vectors.shape
    rank_size = leaf_basis.shape[0]
    leaf_size = near_tiles.shape[1]
    leaf_count = points // leaf_size
    node_count = local_transfer.shape[0]
    peer_count = lax.axis_size("leaf")
    slot_count = far_tiles.shape[0]
    offsets = far_counts.shape[1]
    slot_cap = slot_count // offsets
    device = lax.axis_index("leaf")
    blocks = vectors.reshape(vec_count, leaf_count, leaf_size)
    bases_grid = leaf_basis.reshape(rank_size, leaf_count, leaf_size)
    following = from_behind(vectors, "leaf", -1)
    joined = jnp.concatenate([blocks, following.reshape(vec_count, leaf_count, leaf_size)], axis=1)
    from_cols = jnp.einsum(
        "vnq,npq->vnp",
        jnp.take(joined, near_cols, axis=1),
        near_tiles,
        preferred_element_type=jnp.float32,
    )
    from_rows = jnp.einsum(
        "vnp,npq->vnq",
        jnp.take(blocks, near_rows, axis=1),
        near_tiles,
        preferred_element_type=jnp.float32,
    )
    near_own = (
        jnp.zeros((vec_count, leaf_count, leaf_size), jnp.float32).at[:, near_rows].add(from_cols)
    )
    spread = (
        jnp.zeros((vec_count, 2 * leaf_count, leaf_size), jnp.float32)
        .at[:, near_cols]
        .add(from_rows)
    )
    near_own = near_own + spread[:, :leaf_count]
    near_got = from_behind(spread[:, leaf_count:].astype(jnp.bfloat16), "leaf", 1).astype(
        jnp.float32
    )
    current = jnp.einsum(
        "vnp,knp->nvk", blocks, bases_grid, preferred_element_type=jnp.float32
    ).astype(jnp.bfloat16)
    pieces = [current]
    offset = 0
    level_size = leaf_count
    while level_size > 1:
        lifted = jnp.einsum(
            "nvk,nkr->nvr",
            current,
            local_transfer[offset : offset + level_size],
            preferred_element_type=jnp.float32,
        )
        current = (
            lifted.reshape(level_size // 2, 2, vec_count, rank_size)
            .sum(axis=1)
            .astype(jnp.bfloat16)
        )
        offset = offset + level_size
        level_size = level_size // 2
        pieces.append(current)
    node_coefs = jnp.concatenate(pieces, axis=0)
    slot_index = jnp.arange(slot_count, dtype=jnp.int32)
    slot_used = (slot_index % slot_cap < jnp.repeat(far_counts[0], slot_cap)).astype(jnp.bfloat16)
    masked = far_tiles * slot_used[:, None, None]
    row_coefs = jnp.take(node_coefs, far_rows, axis=0)
    tiles_grid = masked.reshape(offsets, slot_cap, rank_size, rank_size)
    coefs_grid = row_coefs.reshape(offsets, slot_cap, vec_count, rank_size)
    rows_grid = far_rows.reshape(offsets, slot_cap)
    cols_grid = far_cols.reshape(offsets, slot_cap)
    target_ids = [rows_grid[0], cols_grid[0]]
    target_terms = [
        jnp.einsum(
            "nvj,nkj->nvk",
            jnp.take(node_coefs, cols_grid[0], axis=0),
            tiles_grid[0],
            preferred_element_type=jnp.float32,
        ),
        jnp.einsum(
            "nvk,nkj->nvj", coefs_grid[0], tiles_grid[0], preferred_element_type=jnp.float32
        ),
    ]
    for step in range(1, offsets):
        got_tiles, got_coefs, got_ids = from_behind(
            (tiles_grid[step], coefs_grid[step], cols_grid[step]), "leaf", step
        )
        col_terms = jnp.einsum(
            "nvk,nkj->nvj", got_coefs, got_tiles, preferred_element_type=jnp.float32
        )
        back_terms = jnp.einsum(
            "nvj,nkj->nvk",
            jnp.take(node_coefs, got_ids, axis=0),
            got_tiles,
            preferred_element_type=jnp.float32,
        )
        row_terms = from_behind(back_terms, "leaf", -step)
        target_ids = target_ids + [rows_grid[step], got_ids]
        target_terms = target_terms + [row_terms, col_terms]
    far_nodes = (
        jnp.zeros((node_count, vec_count, rank_size), jnp.float32)
        .at[jnp.concatenate(target_ids)]
        .add(jnp.concatenate(target_terms, axis=0))
    )
    root_coef = node_coefs[node_count - 1].astype(jnp.float32)
    root_lift = jnp.dot(
        node_coefs[node_count - 1],
        local_transfer[node_count - 1],
        preferred_element_type=jnp.float32,
    )
    top_levels = peer_count.bit_length() - 1
    heap_node = peer_count + device
    couplings = []
    own_coef = root_coef
    own_lift = root_lift
    for height in range(top_levels):
        node_here = heap_node >> height
        other_coef, other_lift = from_partner((own_coef, own_lift), "leaf", height)
        coupling_tile = pick_tile(top_couple, (node_here >> 1) - 1)
        to_left = jnp.dot(other_coef, coupling_tile.T, precision=highest)
        to_right = jnp.dot(other_coef, coupling_tile, precision=highest)
        couplings.append(jnp.where(node_here % 2 == 0, to_left, to_right))
        if height + 1 < top_levels:
            own_coef = own_lift + other_lift
            own_lift = jnp.dot(
                own_coef, pick_tile(top_transfer, (node_here >> 1) - 2), precision=highest
            )
    going_down = couplings[top_levels - 1]
    for height in range(top_levels - 2, -1, -1):
        if height == 0:
            transfer = local_transfer[node_count - 1].astype(jnp.float32)
        else:
            transfer = pick_tile(top_transfer, (heap_node >> height) - 2)
        going_down = couplings[height] + jnp.dot(going_down, transfer.T, precision=highest)
    current = (far_nodes[node_count - 1] + going_down)[None]
    offset = node_count - 1
    level_size = 1
    while level_size < leaf_count:
        level_size = level_size * 2
        offset = offset - level_size
        parents = jnp.repeat(current, 2, axis=0)
        current = far_nodes[offset : offset + level_size] + jnp.einsum(
            "nvr,nkr->nvk",
            parents,
            local_transfer[offset : offset + level_size].astype(jnp.float32),
            precision=highest,
        )
    leaf_down = current.astype(jnp.bfloat16)
    far_out = jnp.einsum("nvk,knp->vnp", leaf_down, bases_grid, preferred_element_type=jnp.float32)
    product = near_own + near_got + far_out
    return product.reshape(vec_count, points)


def solution(mesh):
    in_specs = (
        P(None, "leaf"),
        P(None, "leaf"),
        P("leaf", None, None),
        P("leaf", None, None),
        P("leaf"),
        P("leaf"),
        P("leaf", None, None),
        P("leaf"),
        P("leaf"),
        P("leaf", None),
        P(),
        P(),
    )
    out_specs = P(None, "leaf")
    return jax.shard_map(body, mesh=mesh, in_specs=in_specs, out_specs=out_specs, check_vma=False)
```

profile of v0, /device:TPU:8, one launch (start us, length us, event | category | flops | bytes accessed | tf_op | source)
XLA Modules:
  0.0 404.0 jit_solution(1463391521428605476)
XLA Ops:
  0.0 3.8 collective-permute-start.42
  13.0 2.4 collective-permute-start.1
  17.5 4.9 %copy.24 = bf16[144,64,64]{2,1,0:T(8,128)(2,1)} copy(bf16[144,64,64]{0,2,1:T(8,128)(2,1)} %param.20) | data formatting | bytes 2359296 | tf_op args[6]
  27.1 3.3 collective-permute-start.9
  33.1 2.4 gather_fusion.1
  38.9 2.1 convolution_dynamic-update-slice_fusion.9
  42.9 2.6 gather_fusion
  45.5 10.5 %fusion.2 = f32[96,64,256]{2,1,0:T(8,128)} fusion(bf16[96,256,256]{2,1,0:T(8,128)(2,1)} %param.17, bf16[96,64,256]{2,1,0:T(8,128)(2,1)} %gather_fusion, pred[96]{0:T(512)(128)(4,1)S(1)} %compare_and_fusion.11), kind=kOutput, calls=%fused_computation.17 | convolution fusion | flops 806879232 | bytes 22020192 | tf_op jit(solution)/shard_map/vnp,npq->vnq/dot_general | solution.py:59
  56.0 2.4 broadcast_in_dim.71
  58.4 19.9 %scatter_fusion = f32[64,64,256]{2,0,1:T(8,128)} fusion(f32[64,64,256]{2,0,1:T(8,128)} %broadcast_in_dim.71, s32[96]{0:T(128)S(1)} %compare_select_fusion.12, f32[96,64,256]{2,1,0:T(8,128)} %fusion.2), kind=kCustom, calls=%fused_computation.12 | custom fusion | flops 1572864 | bytes 18874752 | tf_op jit(solution)/shard_map/scatter-add | solution.py:71
  78.3 2.7 slice.366
  81.0 2.9 collective-permute-start.3
  84.0 3.7 collective-permute-start.4
  87.8 4.1 %collective-permute-start.5 = (s32[16]{0:T(128)S(1)}, s32[16]{0:T(128)S(1)}, u32[]{:S(2)}, u32[]{:S(2)}) collective-permute-start(s32[16]{0:T(128)S(1)} %copy-done.20), channel_id=1, source_target_pairs={{0,5},{1,6},{2,7},{3,8},{4,9},{5,10},{6,11},{7,12},{8,13},{9,14},{... | collective-permute-start | bytes 200 | tf_op jit(solution)/shard_map/ppermute | solution.py:12
  91.9 3.9 collective-permute-start.6
  95.9 3.2 collective-permute-start.7
  99.1 2.2 collective-permute-start.8
  101.3 2.5 collective-permute-start.11
  122.0 2.8 collective-permute-done.38
  128.0 2.4 collective-permute-done.40
  130.4 2.4 collective-permute-start.12
  134.1 3.7 collective-permute-done.41
  137.8 3.9 collective-permute-start.14
  149.8 2.8 collective-permute-start.18
  153.9 2.9 collective-permute-done.15
  156.8 5.2 %collective-permute-start.21 = (bf16[16,64,64]{2,1,0:T(8,128)(2,1)S(1)}, bf16[16,64,64]{2,1,0:T(8,128)(2,1)S(1)}, u32[]{:S(2)}, u32[]{:S(2)}) collective-permute-start(bf16[16,64,64]{2,1,0:T(8,128)(2,1)S(1)} %copy-done.9), channel_id=1, source_target_pairs={{0,5},{1,6},{2,7},{3,8},{4,9},{5,10},{6,11},{7,12},{8,13},{9,14},{... | collective-permute-start | bytes 393224 | tf_op jit(solution)/shard_map/ppermute | solution.py:12
  163.7 2.2 collective-permute-start.24
  166.3 11.2 %collective-permute-start.27 = (bf16[16,64,64]{2,1,0:T(8,128)(2,1)S(1)}, bf16[16,64,64]{2,1,0:T(8,128)(2,1)S(1)}, u32[]{:S(2)}, u32[]{:S(2)}) collective-permute-start(bf16[16,64,64]{2,1,0:T(8,128)(2,1)S(1)} %copy-done.7), channel_id=1, source_target_pairs={{0,7},{1,8},{2,9},{3,10},{4,11},{5,12},{6,13},{7,14},{8,15},{9,16}... | collective-permute-start | bytes 393224 | tf_op jit(solution)/shard_map/ppermute | solution.py:12
  177.9 3.2 collective-permute-start.30
  183.7 2.6 collective-permute-done.30
  186.3 4.0 collective-permute-start.17
  193.3 4.6 %collective-permute-start.20 = (bf16[16,64,64]{2,1,0:T(8,128)(2,1)S(1)}, bf16[16,64,64]{2,1,0:T(8,128)(2,1)S(1)}, u32[]{:S(2)}, u32[]{:S(2)}) collective-permute-start(bf16[16,64,64]{2,1,0:T(8,128)(2,1)S(1)} %copy-done.14), channel_id=1, source_target_pairs={{0,4},{1,5},{2,6},{3,7},{4,8},{5,9},{6,10},{7,11},{8,12},{9,13},{1... | collective-permute-start | bytes 393224 | tf_op jit(solution)/shard_map/ppermute | solution.py:12
  200.0 5.1 %collective-permute-done.13 = f32[16,64,64]{2,1,0:T(8,128)S(1)} collective-permute-done((f32[16,64,64]{2,1,0:T(8,128)S(1)}, f32[16,64,64]{2,1,0:T(8,128)S(1)}, u32[]{:S(2)}, u32[]{:S(2)}) %collective-permute-start.13) | collective-permute-done | bytes 262176 | tf_op jit(solution)/shard_map/ppermute | solution.py:12
  205.1 4.6 %collective-permute-start.16 = (f32[16,64,64]{2,1,0:T(8,128)S(1)}, f32[16,64,64]{2,1,0:T(8,128)S(1)}, u32[]{:S(2)}, u32[]{:S(2)}) collective-permute-start(f32[16,64,64]{2,1,0:T(8,128)S(1)} %fusion.38), channel_id=1, source_target_pairs={{3,0},{4,1},{5,2},{6,3},{7,4},{8,5},{9,6},{10,7},{11,8},{12,9},{13... | collective-permute-start | bytes 786440 | tf_op jit(solution)/shard_map/ppermute | solution.py:12
  210.5 6.8 %collective-permute-start.23 = (bf16[16,64,64]{2,1,0:T(8,128)(2,1)S(1)}, bf16[16,64,64]{2,1,0:T(8,128)(2,1)S(1)}, u32[]{:S(2)}, u32[]{:S(2)}) collective-permute-start(bf16[16,64,64]{2,1,0:T(8,128)(2,1)S(1)} %copy-done.13), channel_id=1, source_target_pairs={{0,5},{1,6},{2,7},{3,8},{4,9},{5,10},{6,11},{7,12},{8,13},{9,14},{... | collective-permute-start | bytes 393224 | tf_op jit(solution)/shard_map/ppermute | solution.py:12
  218.3 6.4 %collective-permute-done.16 = f32[16,64,64]{2,1,0:T(8,128)S(1)} collective-permute-done((f32[16,64,64]{2,1,0:T(8,128)S(1)}, f32[16,64,64]{2,1,0:T(8,128)S(1)}, u32[]{:S(2)}, u32[]{:S(2)}) %collective-permute-start.16) | collective-permute-done | bytes 262176 | tf_op jit(solution)/shard_map/ppermute | solution.py:12
  227.4 10.3 %collective-permute-start.26 = (bf16[16,64,64]{2,1,0:T(8,128)(2,1)S(1)}, bf16[16,64,64]{2,1,0:T(8,128)(2,1)S(1)}, u32[]{:S(2)}, u32[]{:S(2)}) collective-permute-start(bf16[16,64,64]{2,1,0:T(8,128)(2,1)S(1)} %copy-done.12), channel_id=1, source_target_pairs={{0,6},{1,7},{2,8},{3,9},{4,10},{5,11},{6,12},{7,13},{8,14},{9,15},... | collective-permute-start | bytes 393224 | tf_op jit(solution)/shard_map/ppermute | solution.py:12
  242.7 17.6 %collective-permute-start.29 = (bf16[16,64,64]{2,1,0:T(8,128)(2,1)S(1)}, bf16[16,64,64]{2,1,0:T(8,128)(2,1)S(1)}, u32[]{:S(2)}, u32[]{:S(2)}) collective-permute-start(bf16[16,64,64]{2,1,0:T(8,128)(2,1)S(1)} %copy-done.11), channel_id=1, source_target_pairs={{0,7},{1,8},{2,9},{3,10},{4,11},{5,12},{6,13},{7,14},{8,15},{9,16}... | collective-permute-start | bytes 393224 | tf_op jit(solution)/shard_map/ppermute | solution.py:12
  264.1 8.7 %collective-permute-start.32 = (bf16[16,64,64]{2,1,0:T(8,128)(2,1)S(1)}, bf16[16,64,64]{2,1,0:T(8,128)(2,1)S(1)}, u32[]{:S(2)}, u32[]{:S(2)}) collective-permute-start(bf16[16,64,64]{2,1,0:T(8,128)(2,1)S(1)} %copy-done.10), channel_id=1, source_target_pairs={{0,8},{1,9},{2,10},{3,11},{4,12},{5,13},{6,14},{7,15},{8,16},{9,17... | collective-permute-start | bytes 393224 | tf_op jit(solution)/shard_map/ppermute | solution.py:12
  273.9 10.6 %collective-permute-done.25 = f32[16,64,64]{2,1,0:T(8,128)S(1)} collective-permute-done((f32[16,64,64]{2,1,0:T(8,128)S(1)}, f32[16,64,64]{2,1,0:T(8,128)S(1)}, u32[]{:S(2)}, u32[]{:S(2)}) %collective-permute-start.25) | collective-permute-done | bytes 262176 | tf_op jit(solution)/shard_map/ppermute | solution.py:12
  290.2 16.9 %collective-permute-done.28 = f32[16,64,64]{2,1,0:T(8,128)S(1)} collective-permute-done((f32[16,64,64]{2,1,0:T(8,128)S(1)}, f32[16,64,64]{2,1,0:T(8,128)S(1)}, u32[]{:S(2)}, u32[]{:S(2)}) %collective-permute-start.28) | collective-permute-done | bytes 262176 | tf_op jit(solution)/shard_map/ppermute | solution.py:12
  311.0 7.2 %collective-permute-done.31 = f32[16,64,64]{2,1,0:T(8,128)S(1)} collective-permute-done((f32[16,64,64]{2,1,0:T(8,128)S(1)}, f32[16,64,64]{2,1,0:T(8,128)S(1)}, u32[]{:S(2)}, u32[]{:S(2)}) %collective-permute-start.31) | collective-permute-done | bytes 262176 | tf_op jit(solution)/shard_map/ppermute | solution.py:12
  320.3 29.8 %scatter_fusion.1 = f32[63,64,64]{2,1,0:T(8,128)S(1)} fusion(f32[63,64,64]{2,1,0:T(8,128)S(1)} %broadcast_in_dim.76, s32[288]{0:T(512)S(1)} %fusion.167, f32[288,64,64]{2,1,0:T(8,128)} %convolution_dynamic-update-slice_fusion.1), kind=kCustom, calls=%fused_computation.13 | custom fusion | flops 1179648 | bytes 14156928 | tf_op jit(solution)/shard_map/scatter-add | solution.py:138
  360.4 4.2 %gather_fusion.2 = bf16[96,64,256]{2,1,0:T(8,128)(2,1)} fusion(bf16[64,64,256]{2,0,1:T(8,128)(2,1)} %pad_maximum_fusion, s32[1024]{0:T(1024)S(1)} %get-tuple-element.56), kind=kCustom, calls=%fused_computation.11 | custom fusion | bytes 6291840 | tf_op jit(solution)/shard_map/jit(_take)/gather | solution.py:55
  364.6 12.1 %fusion = f32[96,64,256]{2,1,0:T(8,128)} fusion(bf16[96,256,256]{2,1,0:T(8,128)(2,1)} %param.17, bf16[96,64,256]{2,1,0:T(8,128)(2,1)} %gather_fusion.2, pred[96]{0:T(512)(128)(4,1)S(1)} %copy-done.18), kind=kOutput, calls=%fused_computation.15 | convolution fusion | flops 806879232 | bytes 22020192 | tf_op jit(solution)/shard_map/vnq,npq->vnp/dot_general | solution.py:53
  376.7 4.4 %fusion.8 = f32[64,32,256]{2,0,1:T(8,128)} fusion(f32[64,64,256]{2,0,1:T(8,128)} %scatter_fusion, bf16[64,32,256]{2,0,1:T(8,128)(2,1)} %collective-permute-done, bf16[8,32,8,256]{3,2,1,0:T(8,128)(2,1)} %bitcast.194, f32[32,64,64]{2,1,0:T(8,128)} %fusion.22, f32[63,64,64]{2,1,0:T(8,128)S(1)} %scatter_fusion.1), kind=kOutput, calls=%fused_computation.26 | convolution fusion | flops 68943872 | bytes 7864320 | tf_op jit(solution)/shard_map/nvk,knp->vnp/dot_general | solution.py:184
  381.1 19.8 %scatter_fusion.2 = f32[64,32,256]{2,0,1:T(8,128)} fusion(f32[64,32,256]{2,0,1:T(8,128)} %fusion.8, s32[96]{0:T(128)S(1)} %compare_select_fusion.11, f32[96,64,256]{2,1,0:T(8,128)} %fusion), kind=kCustom, calls=%fused_computation.14 | custom fusion | flops 1572864 | bytes 18874752 | tf_op jit(solution)/shard_map/scatter-add | solution.py:66
  400.9 3.1 copy.32
  (222 shorter events, 101.7 us)
Async XLA Ops:
  0.0 116.7 %copy-start = (f32[31,64,64]{2,1,0:T(8,128)S(1)}, f32[31,64,64]{2,1,0:T(8,128)}, u32[]{:S(2)}) copy-start(f32[31,64,64]{2,1,0:T(8,128)} %param.25) | copy-start | bytes 1523716
  0.0 357.5 %collective-permute-start.42 = (bf16[64,8192]{1,0:T(8,128)(2,1)}, bf16[64,8192]{1,0:T(8,128)(2,1)}, u32[]{:S(2)}, u32[]{:S(2)}) collective-permute-start(bf16[64,8192]{1,0:T(8,128)(2,1)} %param.14), channel_id=1, source_target_pairs={{1,0},{2,1},{3,2},{4,3},{5,4},{6,5},{7,6},{8,7},{9,8},{10,9},{11,1... | collective-permute-start | bytes 3145736 | tf_op jit(solution)/shard_map/ppermute | solution.py:12
  12.4 101.2 %collective-permute-start.34 = (f32[64,64]{1,0:T(8,128)S(1)}, f32[64,64]{1,0:T(8,128)S(1)}, u32[]{:S(2)}, u32[]{:S(2)}) collective-permute-start(f32[64,64]{1,0:T(8,128)S(1)} %fusion.146), channel_id=1, source_target_pairs={{0,1},{1,0},{2,3},{3,2},{4,5},{5,4},{6,7},{7,6},{8,9},{9,8},{10,11... | collective-permute-start | bytes 49160 | tf_op jit(solution)/shard_map/ppermute | solution.py:18
  13.0 68.0 %collective-permute-start.1 = (s32[16]{0:T(128)}, s32[16]{0:T(128)S(1)}, u32[]{:S(2)}, u32[]{:S(2)}) collective-permute-start(s32[16]{0:T(128)} %get-tuple-element.30), channel_id=1, source_target_pairs={{0,1},{1,2},{2,3},{3,4},{4,5},{5,6},{6,7},{7,8},{8,9},{9,10},{10,1... | collective-permute-start | bytes 200 | tf_op jit(solution)/shard_map/ppermute | solution.py:12
  15.4 68.5 %collective-permute-start.2 = (s32[16]{0:T(128)}, s32[16]{0:T(128)S(1)}, u32[]{:S(2)}, u32[]{:S(2)}) collective-permute-start(s32[16]{0:T(128)} %get-tuple-element.29), channel_id=1, source_target_pairs={{0,2},{1,3},{2,4},{3,5},{4,6},{5,7},{6,8},{7,9},{8,10},{9,11},{10,... | collective-permute-start | bytes 200 | tf_op jit(solution)/shard_map/ppermute | solution.py:12
  27.1 119.4 %collective-permute-start.9 = (bf16[16,64,64]{2,1,0:T(8,128)(2,1)}, bf16[16,64,64]{2,1,0:T(8,128)(2,1)}, u32[]{:S(2)}, u32[]{:S(2)}) collective-permute-start(bf16[16,64,64]{2,1,0:T(8,128)(2,1)} %get-tuple-element.23), channel_id=1, source_target_pairs={{0,1},{1,2},{2,3},{3,4},{4,5},{5,6},{6,7},{7,8},{8,9},{9,10},{10,1... | collective-permute-start | bytes 393224 | tf_op jit(solution)/shard_map/ppermute | solution.py:12
  81.0 6.7 %collective-permute-start.3 = (s32[16]{0:T(128)S(1)}, s32[16]{0:T(128)S(1)}, u32[]{:S(2)}, u32[]{:S(2)}) collective-permute-start(s32[16]{0:T(128)S(1)} %copy-done.22), channel_id=1, source_target_pairs={{0,3},{1,4},{2,5},{3,6},{4,7},{5,8},{6,9},{7,10},{8,11},{9,12},{10... | collective-permute-start | bytes 200 | tf_op jit(solution)/shard_map/ppermute | solution.py:12
  84.0 7.9 %collective-permute-start.4 = (s32[16]{0:T(128)S(1)}, s32[16]{0:T(128)S(1)}, u32[]{:S(2)}, u32[]{:S(2)}) collective-permute-start(s32[16]{0:T(128)S(1)} %copy-done.21), channel_id=1, source_target_pairs={{0,4},{1,5},{2,6},{3,7},{4,8},{5,9},{6,10},{7,11},{8,12},{9,13},{1... | collective-permute-start | bytes 200 | tf_op jit(solution)/shard_map/ppermute | solution.py:12
  87.8 8.1 %collective-permute-start.5 = (s32[16]{0:T(128)S(1)}, s32[16]{0:T(128)S(1)}, u32[]{:S(2)}, u32[]{:S(2)}) collective-permute-start(s32[16]{0:T(128)S(1)} %copy-done.20), channel_id=1, source_target_pairs={{0,5},{1,6},{2,7},{3,8},{4,9},{5,10},{6,11},{7,12},{8,13},{9,14},{... | collective-permute-start | bytes 200 | tf_op jit(solution)/shard_map/ppermute | solution.py:12
  91.9 7.2 %collective-permute-start.6 = (s32[16]{0:T(128)S(1)}, s32[16]{0:T(128)S(1)}, u32[]{:S(2)}, u32[]{:S(2)}) collective-permute-start(s32[16]{0:T(128)S(1)} %get-tuple-element.25), channel_id=1, source_target_pairs={{0,6},{1,7},{2,8},{3,9},{4,10},{5,11},{6,12},{7,13},{8,14},{9,15},... | collective-permute-start | bytes 200 | tf_op jit(solution)/shard_map/ppermute | solution.py:12
  95.9 5.4 %collective-permute-start.7 = (s32[16]{0:T(128)S(1)}, s32[16]{0:T(128)S(1)}, u32[]{:S(2)}, u32[]{:S(2)}) collective-permute-start(s32[16]{0:T(128)S(1)} %get-tuple-element.32), channel_id=1, source_target_pairs={{0,7},{1,8},{2,9},{3,10},{4,11},{5,12},{6,13},{7,14},{8,15},{9,16}... | collective-permute-start | bytes 200 | tf_op jit(solution)/shard_map/ppermute | solution.py:12
  99.1 5.4 %collective-permute-start.8 = (s32[16]{0:T(128)S(1)}, s32[16]{0:T(128)S(1)}, u32[]{:S(2)}, u32[]{:S(2)}) collective-permute-start(s32[16]{0:T(128)S(1)} %get-tuple-element.24), channel_id=1, source_target_pairs={{0,8},{1,9},{2,10},{3,11},{4,12},{5,13},{6,14},{7,15},{8,16},{9,17... | collective-permute-start | bytes 200 | tf_op jit(solution)/shard_map/ppermute | solution.py:12
  101.3 92.0 %collective-permute-start.11 = (bf16[16,64,64]{2,1,0:T(8,128)(2,1)}, bf16[16,64,64]{2,1,0:T(8,128)(2,1)}, u32[]{:S(2)}, u32[]{:S(2)}) collective-permute-start(bf16[16,64,64]{2,1,0:T(8,128)(2,1)} %get-tuple-element.15), channel_id=1, source_target_pairs={{0,1},{1,2},{2,3},{3,4},{4,5},{5,6},{6,7},{7,8},{8,9},{9,10},{10,1... | collective-permute-start | bytes 393224 | tf_op jit(solution)/shard_map/ppermute | solution.py:12
  104.5 10.3 %collective-permute-start.33 = (f32[64,64]{1,0:T(8,128)S(1)}, f32[64,64]{1,0:T(8,128)S(1)}, u32[]{:S(2)}, u32[]{:S(2)}) collective-permute-start(f32[64,64]{1,0:T(8,128)S(1)} %convert_element_type.57), channel_id=1, source_target_pairs={{0,1},{1,0},{2,3},{3,2},{4,5},{5,4},{6,7},{7,6},{8,9},{9,8},{10,11... | collective-permute-start | bytes 49160 | tf_op jit(solution)/shard_map/ppermute | solution.py:18
  113.5 52.7 %copy-start.7 = (bf16[16,64,64]{2,1,0:T(8,128)(2,1)S(1)}, bf16[16,64,64]{2,1,0:T(8,128)(2,1)}, u32[]{:S(2)}) copy-start(bf16[16,64,64]{2,1,0:T(8,128)(2,1)} %get-tuple-element.17) | copy-start | bytes 393220
  113.5 64.3 %copy-start.6 = (bf16[16,64,64]{2,1,0:T(8,128)(2,1)S(1)}, bf16[16,64,64]{2,1,0:T(8,128)(2,1)}, u32[]{:S(2)}) copy-start(bf16[16,64,64]{2,1,0:T(8,128)(2,1)} %get-tuple-element.16) | copy-start | bytes 393220
  113.6 7.2 %collective-permute-start.35 = (f32[64,64]{1,0:T(8,128)S(1)}, f32[64,64]{1,0:T(8,128)S(1)}, u32[]{:S(2)}, u32[]{:S(2)}) collective-permute-start(f32[64,64]{1,0:T(8,128)S(1)} %add.213), channel_id=1, source_target_pairs={{0,2},{1,3},{2,0},{3,1},{4,6},{5,7},{6,4},{7,5},{8,10},{9,11},{10,... | collective-permute-start | bytes 49160 | tf_op jit(solution)/shard_map/ppermute | solution.py:18
  114.8 4.0 collective-permute-start.36
  118.8 7.6 %collective-permute-start.37 = (f32[64,64]{1,0:T(8,128)S(1)}, f32[64,64]{1,0:T(8,128)S(1)}, u32[]{:S(2)}, u32[]{:S(2)}) collective-permute-start(f32[64,64]{1,0:T(8,128)S(1)} %add.217), channel_id=1, source_target_pairs={{0,4},{1,5},{2,6},{3,7},{4,0},{5,1},{6,2},{7,3},{8,12},{9,13},{10,... | collective-permute-start | bytes 49160 | tf_op jit(solution)/shard_map/ppermute | solution.py:18
  120.8 4.0 collective-permute-start.38
  124.8 8.1 %collective-permute-start.39 = (f32[64,64]{1,0:T(8,128)S(1)}, f32[64,64]{1,0:T(8,128)S(1)}, u32[]{:S(2)}, u32[]{:S(2)}) collective-permute-start(f32[64,64]{1,0:T(8,128)S(1)} %add.221), channel_id=1, source_target_pairs={{0,8},{1,9},{2,10},{3,11},{4,12},{5,13},{6,14},{7,15},{8,0},{9,1},... | collective-permute-start | bytes 49160 | tf_op jit(solution)/shard_map/ppermute | solution.py:18
  126.4 4.0 collective-permute-start.40
  130.4 19.4 %collective-permute-start.12 = (bf16[16,64,64]{2,1,0:T(8,128)(2,1)}, bf16[16,64,64]{2,1,0:T(8,128)(2,1)S(1)}, u32[]{:S(2)}, u32[]{:S(2)}) collective-permute-start(bf16[16,64,64]{2,1,0:T(8,128)(2,1)} %get-tuple-element.22), channel_id=1, source_target_pairs={{0,2},{1,3},{2,4},{3,5},{4,6},{5,7},{6,8},{7,9},{8,10},{9,11},{10,... | collective-permute-start | bytes 393224 | tf_op jit(solution)/shard_map/ppermute | solution.py:12
  132.9 4.9 %collective-permute-start.41 = (f32[64,64]{1,0:T(8,128)S(1)}, f32[64,64]{1,0:T(8,128)S(1)}, u32[]{:S(2)}, u32[]{:S(2)}) collective-permute-start(f32[64,64]{1,0:T(8,128)S(1)} %add.225), channel_id=1, source_target_pairs={{0,16},{1,17},{2,18},{3,19},{4,20},{5,21},{6,22},{7,23},{8,24},{9,... | collective-permute-start | bytes 49160 | tf_op jit(solution)/shard_map/ppermute | solution.py:18
  137.8 72.7 %collective-permute-start.14 = (bf16[16,64,64]{2,1,0:T(8,128)(2,1)}, bf16[16,64,64]{2,1,0:T(8,128)(2,1)S(1)}, u32[]{:S(2)}, u32[]{:S(2)}) collective-permute-start(bf16[16,64,64]{2,1,0:T(8,128)(2,1)} %get-tuple-element.14), channel_id=1, source_target_pairs={{0,2},{1,3},{2,4},{3,5},{4,6},{5,7},{6,8},{7,9},{8,10},{9,11},{10,... | collective-permute-start | bytes 393224 | tf_op jit(solution)/shard_map/ppermute | solution.py:12
  146.5 10.3 %collective-permute-start.15 = (bf16[16,64,64]{2,1,0:T(8,128)(2,1)}, bf16[16,64,64]{2,1,0:T(8,128)(2,1)S(1)}, u32[]{:S(2)}, u32[]{:S(2)}) collective-permute-start(bf16[16,64,64]{2,1,0:T(8,128)(2,1)} %get-tuple-element.21), channel_id=1, source_target_pairs={{0,3},{1,4},{2,5},{3,6},{4,7},{5,8},{6,9},{7,10},{8,11},{9,12},{10... | collective-permute-start | bytes 393224 | tf_op jit(solution)/shard_map/ppermute | solution.py:12
  149.8 13.9 %collective-permute-start.18 = (bf16[16,64,64]{2,1,0:T(8,128)(2,1)}, bf16[16,64,64]{2,1,0:T(8,128)(2,1)S(1)}, u32[]{:S(2)}, u32[]{:S(2)}) collective-permute-start(bf16[16,64,64]{2,1,0:T(8,128)(2,1)} %get-tuple-element.20), channel_id=1, source_target_pairs={{0,4},{1,5},{2,6},{3,7},{4,8},{5,9},{6,10},{7,11},{8,12},{9,13},{1... | collective-permute-start | bytes 393224 | tf_op jit(solution)/shard_map/ppermute | solution.py:12
  156.8 9.5 %collective-permute-start.21 = (bf16[16,64,64]{2,1,0:T(8,128)(2,1)S(1)}, bf16[16,64,64]{2,1,0:T(8,128)(2,1)S(1)}, u32[]{:S(2)}, u32[]{:S(2)}) collective-permute-start(bf16[16,64,64]{2,1,0:T(8,128)(2,1)S(1)} %copy-done.9), channel_id=1, source_target_pairs={{0,5},{1,6},{2,7},{3,8},{4,9},{5,10},{6,11},{7,12},{8,13},{9,14},{... | collective-permute-start | bytes 393224 | tf_op jit(solution)/shard_map/ppermute | solution.py:12
  163.7 14.1 %collective-permute-start.24 = (bf16[16,64,64]{2,1,0:T(8,128)(2,1)S(1)}, bf16[16,64,64]{2,1,0:T(8,128)(2,1)S(1)}, u32[]{:S(2)}, u32[]{:S(2)}) collective-permute-start(bf16[16,64,64]{2,1,0:T(8,128)(2,1)S(1)} %copy-done.8), channel_id=1, source_target_pairs={{0,6},{1,7},{2,8},{3,9},{4,10},{5,11},{6,12},{7,13},{8,14},{9,15},... | collective-permute-start | bytes 393224 | tf_op jit(solution)/shard_map/ppermute | solution.py:12
  166.3 15.1 %collective-permute-start.27 = (bf16[16,64,64]{2,1,0:T(8,128)(2,1)S(1)}, bf16[16,64,64]{2,1,0:T(8,128)(2,1)S(1)}, u32[]{:S(2)}, u32[]{:S(2)}) collective-permute-start(bf16[16,64,64]{2,1,0:T(8,128)(2,1)S(1)} %copy-done.7), channel_id=1, source_target_pairs={{0,7},{1,8},{2,9},{3,10},{4,11},{5,12},{6,13},{7,14},{8,15},{9,16}... | collective-permute-start | bytes 393224 | tf_op jit(solution)/shard_map/ppermute | solution.py:12
  177.9 8.4 %collective-permute-start.30 = (bf16[16,64,64]{2,1,0:T(8,128)(2,1)S(1)}, bf16[16,64,64]{2,1,0:T(8,128)(2,1)S(1)}, u32[]{:S(2)}, u32[]{:S(2)}) collective-permute-start(bf16[16,64,64]{2,1,0:T(8,128)(2,1)S(1)} %copy-done.6), channel_id=1, source_target_pairs={{0,8},{1,9},{2,10},{3,11},{4,12},{5,13},{6,14},{7,15},{8,16},{9,17... | collective-permute-start | bytes 393224 | tf_op jit(solution)/shard_map/ppermute | solution.py:12
  181.4 9.2 %collective-permute-start.10 = (f32[16,64,64]{2,1,0:T(8,128)S(1)}, f32[16,64,64]{2,1,0:T(8,128)S(1)}, u32[]{:S(2)}, u32[]{:S(2)}) collective-permute-start(f32[16,64,64]{2,1,0:T(8,128)S(1)} %fusion.42), channel_id=1, source_target_pairs={{1,0},{2,1},{3,2},{4,3},{5,4},{6,5},{7,6},{8,7},{9,8},{10,9},{11,1... | collective-permute-start | bytes 786440 | tf_op jit(solution)/shard_map/ppermute | solution.py:12
  186.3 56.5 %copy-start.11 = (bf16[16,64,64]{2,1,0:T(8,128)(2,1)S(1)}, bf16[16,64,64]{2,1,0:T(8,128)(2,1)}, u32[]{:S(2)}) copy-start(bf16[16,64,64]{2,1,0:T(8,128)(2,1)} %get-tuple-element.9) | copy-start | bytes 393220
  186.3 41.2 %collective-permute-start.17 = (bf16[16,64,64]{2,1,0:T(8,128)(2,1)S(1)}, bf16[16,64,64]{2,1,0:T(8,128)(2,1)S(1)}, u32[]{:S(2)}, u32[]{:S(2)}) collective-permute-start(bf16[16,64,64]{2,1,0:T(8,128)(2,1)S(1)} %copy-done.15), channel_id=1, source_target_pairs={{0,3},{1,4},{2,5},{3,6},{4,7},{5,8},{6,9},{7,10},{8,11},{9,12},{10... | collective-permute-start | bytes 393224 | tf_op jit(solution)/shard_map/ppermute | solution.py:12
  190.6 14.5 %collective-permute-start.13 = (f32[16,64,64]{2,1,0:T(8,128)S(1)}, f32[16,64,64]{2,1,0:T(8,128)S(1)}, u32[]{:S(2)}, u32[]{:S(2)}) collective-permute-start(f32[16,64,64]{2,1,0:T(8,128)S(1)} %fusion.40), channel_id=1, source_target_pairs={{2,0},{3,1},{4,2},{5,3},{6,4},{7,5},{8,6},{9,7},{10,8},{11,9},{12,... | collective-permute-start | bytes 786440 | tf_op jit(solution)/shard_map/ppermute | solution.py:12
  193.3 70.8 %copy-start.10 = (bf16[16,64,64]{2,1,0:T(8,128)(2,1)S(1)}, bf16[16,64,64]{2,1,0:T(8,128)(2,1)}, u32[]{:S(2)}) copy-start(bf16[16,64,64]{2,1,0:T(8,128)(2,1)} %get-tuple-element.8) | copy-start | bytes 393220
  193.3 49.4 %collective-permute-start.20 = (bf16[16,64,64]{2,1,0:T(8,128)(2,1)S(1)}, bf16[16,64,64]{2,1,0:T(8,128)(2,1)S(1)}, u32[]{:S(2)}, u32[]{:S(2)}) collective-permute-start(bf16[16,64,64]{2,1,0:T(8,128)(2,1)S(1)} %copy-done.14), channel_id=1, source_target_pairs={{0,4},{1,5},{2,6},{3,7},{4,8},{5,9},{6,10},{7,11},{8,12},{9,13},{1... | collective-permute-start | bytes 393224 | tf_op jit(solution)/shard_map/ppermute | solution.py:12
  205.1 19.6 %collective-permute-start.16 = (f32[16,64,64]{2,1,0:T(8,128)S(1)}, f32[16,64,64]{2,1,0:T(8,128)S(1)}, u32[]{:S(2)}, u32[]{:S(2)}) collective-permute-start(f32[16,64,64]{2,1,0:T(8,128)S(1)} %fusion.38), channel_id=1, source_target_pairs={{3,0},{4,1},{5,2},{6,3},{7,4},{8,5},{9,6},{10,7},{11,8},{12,9},{13... | collective-permute-start | bytes 786440 | tf_op jit(solution)/shard_map/ppermute | solution.py:12
  210.5 53.6 %collective-permute-start.23 = (bf16[16,64,64]{2,1,0:T(8,128)(2,1)S(1)}, bf16[16,64,64]{2,1,0:T(8,128)(2,1)S(1)}, u32[]{:S(2)}, u32[]{:S(2)}) collective-permute-start(bf16[16,64,64]{2,1,0:T(8,128)(2,1)S(1)} %copy-done.13), channel_id=1, source_target_pairs={{0,5},{1,6},{2,7},{3,8},{4,9},{5,10},{6,11},{7,12},{8,13},{9,14},{... | collective-permute-start | bytes 393224 | tf_op jit(solution)/shard_map/ppermute | solution.py:12
  224.7 15.3 %collective-permute-start.19 = (f32[16,64,64]{2,1,0:T(8,128)S(1)}, f32[16,64,64]{2,1,0:T(8,128)S(1)}, u32[]{:S(2)}, u32[]{:S(2)}) collective-permute-start(f32[16,64,64]{2,1,0:T(8,128)S(1)} %fusion.36), channel_id=1, source_target_pairs={{4,0},{5,1},{6,2},{7,3},{8,4},{9,5},{10,6},{11,7},{12,8},{13,9},{1... | collective-permute-start | bytes 786440 | tf_op jit(solution)/shard_map/ppermute | solution.py:12
  227.4 59.8 %collective-permute-start.26 = (bf16[16,64,64]{2,1,0:T(8,128)(2,1)S(1)}, bf16[16,64,64]{2,1,0:T(8,128)(2,1)S(1)}, u32[]{:S(2)}, u32[]{:S(2)}) collective-permute-start(bf16[16,64,64]{2,1,0:T(8,128)(2,1)S(1)} %copy-done.12), channel_id=1, source_target_pairs={{0,6},{1,7},{2,8},{3,9},{4,10},{5,11},{6,12},{7,13},{8,14},{9,15},... | collective-permute-start | bytes 393224 | tf_op jit(solution)/shard_map/ppermute | solution.py:12
  240.0 21.4 %collective-permute-start.22 = (f32[16,64,64]{2,1,0:T(8,128)S(1)}, f32[16,64,64]{2,1,0:T(8,128)S(1)}, u32[]{:S(2)}, u32[]{:S(2)}) collective-permute-start(f32[16,64,64]{2,1,0:T(8,128)S(1)} %fusion.34), channel_id=1, source_target_pairs={{5,0},{6,1},{7,2},{8,3},{9,4},{10,5},{11,6},{12,7},{13,8},{14,9},{... | collective-permute-start | bytes 786440 | tf_op jit(solution)/shard_map/ppermute | solution.py:12
  242.7 67.2 %collective-permute-start.29 = (bf16[16,64,64]{2,1,0:T(8,128)(2,1)S(1)}, bf16[16,64,64]{2,1,0:T(8,128)(2,1)S(1)}, u32[]{:S(2)}, u32[]{:S(2)}) collective-permute-start(bf16[16,64,64]{2,1,0:T(8,128)(2,1)S(1)} %copy-done.11), channel_id=1, source_target_pairs={{0,7},{1,8},{2,9},{3,10},{4,11},{5,12},{6,13},{7,14},{8,15},{9,16}... | collective-permute-start | bytes 393224 | tf_op jit(solution)/shard_map/ppermute | solution.py:12
  261.4 23.1 %collective-permute-start.25 = (f32[16,64,64]{2,1,0:T(8,128)S(1)}, f32[16,64,64]{2,1,0:T(8,128)S(1)}, u32[]{:S(2)}, u32[]{:S(2)}) collective-permute-start(f32[16,64,64]{2,1,0:T(8,128)S(1)} %fusion.32), channel_id=1, source_target_pairs={{6,0},{7,1},{8,2},{9,3},{10,4},{11,5},{12,6},{13,7},{14,8},{15,9},... | collective-permute-start | bytes 786440 | tf_op jit(solution)/shard_map/ppermute | solution.py:12
  264.1 54.9 %collective-permute-start.32 = (bf16[16,64,64]{2,1,0:T(8,128)(2,1)S(1)}, bf16[16,64,64]{2,1,0:T(8,128)(2,1)S(1)}, u32[]{:S(2)}, u32[]{:S(2)}) collective-permute-start(bf16[16,64,64]{2,1,0:T(8,128)(2,1)S(1)} %copy-done.10), channel_id=1, source_target_pairs={{0,8},{1,9},{2,10},{3,11},{4,12},{5,13},{6,14},{7,15},{8,16},{9,17... | collective-permute-start | bytes 393224 | tf_op jit(solution)/shard_map/ppermute | solution.py:12
  284.5 22.6 %collective-permute-start.28 = (f32[16,64,64]{2,1,0:T(8,128)S(1)}, f32[16,64,64]{2,1,0:T(8,128)S(1)}, u32[]{:S(2)}, u32[]{:S(2)}) collective-permute-start(f32[16,64,64]{2,1,0:T(8,128)S(1)} %fusion.30), channel_id=1, source_target_pairs={{7,0},{8,1},{9,2},{10,3},{11,4},{12,5},{13,6},{14,7},{15,8},{16,9}... | collective-permute-start | bytes 786440 | tf_op jit(solution)/shard_map/ppermute | solution.py:12
  287.3 89.5 %collective-permute-start = (bf16[64,32,256]{2,0,1:T(8,128)(2,1)}, bf16[64,32,256]{2,0,1:T(8,128)(2,1)}, u32[]{:S(2)}, u32[]{:S(2)}) collective-permute-start(bf16[64,32,256]{2,0,1:T(8,128)(2,1)} %slice.366), channel_id=1, source_target_pairs={{0,1},{1,2},{2,3},{3,4},{4,5},{5,6},{6,7},{7,8},{8,9},{9,10},{10,1... | collective-permute-start | bytes 3145736 | tf_op jit(solution)/shard_map/ppermute | solution.py:12
  307.1 11.1 %collective-permute-start.31 = (f32[16,64,64]{2,1,0:T(8,128)S(1)}, f32[16,64,64]{2,1,0:T(8,128)S(1)}, u32[]{:S(2)}, u32[]{:S(2)}) collective-permute-start(f32[16,64,64]{2,1,0:T(8,128)S(1)} %fusion.28), channel_id=1, source_target_pairs={{8,0},{9,1},{10,2},{11,3},{12,4},{13,5},{14,6},{15,7},{16,8},{17,9... | collective-permute-start | bytes 786440 | tf_op jit(solution)/shard_map/ppermute | solution.py:12
  (20 other events, 489.7 us)
where the time goes:
time: 409 us; the launch traced here: 404 us
  starting transfers between devices  148 us (36%)
  other arithmetic  75.7 us (19%)
  matrix products  68.4 us (17%)
  waiting for transfers between devices  66 us (16%)
  local copies, waits for them, and re-layouts  44.8 us (11%)
    ppermute x34, starting transfers between devices, from_behind(): lax.ppermute(value, axis, [(source, source + steps) for source in range(i...  139 us
    ppermute x34, waiting for transfers between devices, from_behind(): lax.ppermute(value, axis, [(source, source + steps) for source in range(i...  55.1 us
    scatter-add x1, other arithmetic, body(): far_nodes = jnp.zeros((node_count, vec_count, rank_size), jnp.float32).at...  29.8 us
    scatter-add x1, other arithmetic, body(): spread = jnp.zeros((vec_count, 2 * leaf_count, leaf_size), jnp.float32).a...  19.9 us
    scatter-add x1, other arithmetic, body(): jnp.zeros((vec_count, leaf_count, leaf_size), jnp.float32).at[:, near_rows]  19.8 us
    unnamed x63, local copies, waits for them, and re-layouts  13.2 us
    dot_general x1, matrix products, body(): jnp.einsum('vnq,npq->vnp', jnp.take(joined, near_cols, axis=1), near_tile...  12.1 us
    ppermute x9, waiting for transfers between devices, from_partner(): return lax.ppermute(value, axis, pairs)  10.9 us
  transfers between devices with their start and end apart: 43, of which 14 were waited for; matrix products, arithmetic and copies ran while one was open for 40% of the time, Pallas kernels for 0%

commit v1 on v0

v1 whole, which is shorter than its diff:
```python
import functools

import jax
import jax.numpy as jnp
from jax import lax
from jax.experimental import pallas as pl
from jax.experimental.pallas import tpu as pltpu
from jax.sharding import PartitionSpec as P

f32 = jnp.float32
bf16 = jnp.bfloat16
highest = lax.Precision.HIGHEST
NT = (((1,), (1,)), ((), ()))
VMEM = pl.BlockSpec(memory_space=pltpu.VMEM)
SMEM = pl.BlockSpec(memory_space=pltpu.SMEM)
LIMIT = 56 * 1024 * 1024


def dot(a, b):
    return jnp.dot(a, b, preferred_element_type=f32)


def dot_nt(a, b):
    return lax.dot_general(a, b, NT, preferred_element_type=f32)


def dot_split(a, b):
    high = a.astype(bf16)
    low = (a - high.astype(f32)).astype(bf16)
    rows = a.shape[0]
    both = dot_nt(jnp.concatenate([high, low], axis=0), b)
    return both[:rows] + both[rows:]


def upward_kernel(leaf_count, leaf_size, vec_ref, basis_ref, pairs_ref, coef_ref, root_ref):
    current = []
    for leaf in range(leaf_count):
        span = slice(leaf * leaf_size, (leaf + 1) * leaf_size)
        current.append(dot_nt(vec_ref[:, span], basis_ref[:, span]).astype(bf16))
    offset = 0
    while True:
        for spot, value in enumerate(current):
            coef_ref[offset + spot] = value
        if len(current) == 1:
            break
        parents = []
        for pair in range(len(current) // 2):
            joined = jnp.concatenate([current[2 * pair], current[2 * pair + 1]], axis=1)
            parents.append(dot(joined, pairs_ref[offset // 2 + pair]).astype(bf16))
        offset += len(current)
        current = parents
    root_ref[...] = current[0]


def pack_kernel(
    count, cap, offsets, rows_ref, counts_ref, ids_ref, coef_ref, tiles_ref, coef_out, term_out
):
    me = lax.axis_index("leaf")
    slots = cap * offsets
    for step in range(1, offsets):
        source = lax.rem(me - step + count, count)

        @pl.loop(0, cap // 2)
        def _(pair):
            values = []
            terms = []
            for half in range(2):
                spot = 2 * pair + half
                slot = step * cap + spot
                values.append(coef_ref[ids_ref[source * slots + slot]])
                term = dot(coef_ref[rows_ref[slot]], tiles_ref[slot])
                used = spot < counts_ref[step]
                terms.append(jnp.where(used, term, 0.0).astype(bf16))
            coef_out[step - 1, pair] = jnp.concatenate(values, axis=1)
            term_out[step - 1, pair] = jnp.concatenate(terms, axis=1)


def exchange_kernel(
    count, reach, coef_in, term_in, coef_out, term_out, coef_send, coef_recv, term_send, term_recv
):
    me = lax.axis_index("leaf")
    barrier = pltpu.get_barrier_semaphore()
    for step in range(1, reach + 1):
        for sign in (-1, 1):
            peer = me + sign * step

            @pl.when((peer >= 0) & (peer < count))
            def _(peer=peer):
                pl.semaphore_signal(
                    barrier, inc=1, device_id=(peer,), device_id_type=pl.DeviceIdType.MESH
                )

    pl.semaphore_wait(barrier, jnp.minimum(me, reach) + jnp.minimum(count - 1 - me, reach))

    def back(step):
        return pltpu.make_async_remote_copy(
            src_ref=coef_in.at[step - 1],
            dst_ref=coef_out.at[step - 1],
            send_sem=coef_send.at[step - 1],
            recv_sem=coef_recv.at[step - 1],
            device_id=(me - step,),
            device_id_type=pl.DeviceIdType.MESH,
        )

    def ahead(step):
        return pltpu.make_async_remote_copy(
            src_ref=term_in.at[step - 1],
            dst_ref=term_out.at[step - 1],
            send_sem=term_send.at[step - 1],
            recv_sem=term_recv.at[step - 1],
            device_id=(me + step,),
            device_id_type=pl.DeviceIdType.MESH,
        )

    for step in range(reach, 0, -1):

        @pl.when(me - step >= 0)
        def _(step=step):
            back(step).start()

        @pl.when(me + step < count)
        def _(step=step):
            ahead(step).start()

    for step in range(1, reach + 1):

        @pl.when(me - step >= 0)
        def _(step=step):
            back(step).wait_send()
            ahead(step).wait_recv()

        @pl.when(me + step < count)
        def _(step=step):
            ahead(step).wait_send()
            back(step).wait_recv()


def near_kernel(
    group, steps, leaf_size, points, rows_ref, cols_ref, vec_ref, next_ref, tiles_ref, own_ref, spread_ref, joined, total
):
    step = pl.program_id(0)

    @pl.when(step == 0)
    def _():
        joined[:, :points] = vec_ref[...]
        joined[:, points:] = next_ref[...]
        total[...] = jnp.zeros_like(total)

    for spot in range(group):
        tile = tiles_ref[spot]
        row = pl.ds(pl.multiple_of(rows_ref[step * group + spot] * leaf_size, leaf_size), leaf_size)
        col = pl.ds(pl.multiple_of(cols_ref[step * group + spot] * leaf_size, leaf_size), leaf_size)
        to_row = dot_nt(joined[:, col], tile)
        to_col = dot(joined[:, row], tile)
        total[:, row] += to_row
        total[:, col] += to_col

    @pl.when(step == steps - 1)
    def _():
        own_ref[...] = total[:, :points]
        spread_ref[...] = total[:, points:].astype(bf16)


def downward_kernel(
    count,
    cap,
    offsets,
    leaf_count,
    leaf_size,
    rows_ref,
    cols_ref,
    counts_ref,
    ids_ref,
    coef_ref,
    tiles_ref,
    coef_got,
    term_got,
    roots_ref,
    transfer_ref,
    top_ref,
    couple_ref,
    pairs_ref,
    basis_ref,
    own_ref,
    got_ref,
    out_ref,
    far,
    level,
):
    me = lax.axis_index("leaf")
    slots = cap * offsets
    rank = coef_ref.shape[1]
    far[...] = jnp.zeros_like(far)

    @pl.loop(0, cap)
    def _(spot):
        tile = tiles_ref[spot]
        row = rows_ref[spot]
        col = cols_ref[spot]
        to_row = dot_nt(coef_ref[col], tile)
        to_col = dot(coef_ref[row], tile)

        @pl.when(spot < counts_ref[0])
        def _():
            far[row] += to_row
            far[col] += to_col

    for step in range(1, offsets):

        @pl.when(me + step < count)
        def _(step=step):
            @pl.loop(0, cap // 2)
            def _(pair):
                values = coef_got[step - 1, pair]
                for half in range(2):
                    spot = 2 * pair + half
                    slot = step * cap + spot
                    term = dot_nt(values[:, half * rank : (half + 1) * rank], tiles_ref[slot])
                    far[rows_ref[slot]] += jnp.where(spot < counts_ref[step], term, 0.0)

        @pl.when(me - step >= 0)
        def _(step=step):
            @pl.loop(0, cap // 2)
            def _(pair):
                values = term_got[step - 1, pair].astype(f32)
                for half in range(2):
                    slot = step * cap + 2 * pair + half
                    node = ids_ref[(me - step) * slots + slot]
                    far[node] += values[:, half * rank : (half + 1) * rank]

    for node in range(count // 2):
        left = roots_ref[2 * node]
        right = roots_ref[2 * node + 1]
        joined = jnp.concatenate([left[:, :rank], right[:, :rank]], axis=1)
        lift = jnp.concatenate([left[:, rank:], right[:, rank:]], axis=0)
        level[count // 2 + node] = dot(joined, lift)
        level[count + 2 * node] = left[:, :rank].astype(f32)
        level[count + 2 * node + 1] = right[:, :rank].astype(f32)
    for node in range(count // 2 - 1, 1, -1):
        joined = jnp.concatenate([level[2 * node], level[2 * node + 1]], axis=1)
        level[node] = jnp.dot(joined, top_ref[node - 1], precision=highest, preferred_element_type=f32)
    heights = count.bit_length() - 1
    heap = count + me
    going = None
    for height in range(heights - 1, -1, -1):
        node = heap >> height
        other = level[node ^ 1]
        tile = couple_ref[(node >> 1) - 1]
        turned = jnp.where(node % 2 == 0, tile.T, tile)
        term = jnp.dot(other, turned, precision=highest, preferred_element_type=f32)
        if going is None:
            going = term
        elif height == 0:
            going = term + dot_split(going, transfer_ref[...])
        else:
            lift = transfer_of(top_ref, node - 2, rank)
            going = term + lax.dot_general(going, lift, NT, precision=highest, preferred_element_type=f32)

    offset = far.shape[0] - 1
    current = [far[offset] + going]
    while len(current) < leaf_count:
        offset -= 2 * len(current)
        children = []
        for spot, value in enumerate(current):
            both = dot_split(value, pairs_ref[offset // 2 + spot])
            children.append(far[offset + 2 * spot] + both[:, :rank])
            children.append(far[offset + 2 * spot + 1] + both[:, rank:])
        current = children
    for leaf, value in enumerate(current):
        span = slice(leaf * leaf_size, (leaf + 1) * leaf_size)
        term = dot(value.astype(bf16), basis_ref[:, span])
        out_ref[:, span] = own_ref[:, span] + got_ref[:, span].astype(f32) + term


def transfer_of(top_ref, index, rank):
    start = pl.multiple_of((index % 2) * rank, rank)
    return top_ref[index // 2, pl.ds(start, rank), :]


def body(
    vectors,
    leaf_basis,
    local_transfer,
    near_tiles,
    near_rows,
    near_cols,
    far_tiles,
    far_rows,
    far_cols,
    far_counts,
    top_transfer,
    top_couple,
):
    vec_count, points = vectors.shape
    rank = leaf_basis.shape[0]
    near_count, leaf_size, _ = near_tiles.shape
    leaf_count = points // leaf_size
    nodes = local_transfer.shape[0]
    count = lax.axis_size("leaf")
    slots = far_tiles.shape[0]
    offsets = far_counts.shape[1]
    reach = offsets - 1
    cap = slots // offsets
    counts = far_counts[0]
    params = pltpu.CompilerParams(vmem_limit_bytes=LIMIT)

    following = lax.ppermute(vectors, "leaf", [(source, source - 1) for source in range(1, count)])
    ids = lax.all_gather(far_cols, "leaf", tiled=True)
    pairs = local_transfer[: nodes - 1].reshape(nodes // 2, 2 * rank, rank)
    root_transfer = local_transfer[nodes - 1]

    coefs, root = pl.pallas_call(
        functools.partial(upward_kernel, leaf_count, leaf_size),
        out_shape=[
            jax.ShapeDtypeStruct((nodes, vec_count, rank), bf16),
            jax.ShapeDtypeStruct((vec_count, rank), bf16),
        ],
        in_specs=[VMEM] * 3,
        out_specs=[VMEM] * 2,
        compiler_params=params,
        name="upward",
    )(vectors, leaf_basis, pairs)
    roots = lax.all_gather(jnp.concatenate([root, root_transfer], axis=1), "leaf")

    packed = jax.ShapeDtypeStruct((reach, cap // 2, vec_count, 2 * rank), bf16)
    coef_send, term_send = pl.pallas_call(
        functools.partial(pack_kernel, count, cap, offsets),
        out_shape=[packed, packed],
        in_specs=[SMEM] * 3 + [VMEM] * 2,
        out_specs=[VMEM] * 2,
        compiler_params=params,
        name="pack",
    )(far_rows, counts, ids, coefs, far_tiles)

    group = 8
    steps = near_count // group
    near_own, spread = pl.pallas_call(
        functools.partial(near_kernel, group, steps, leaf_size, points),
        out_shape=[
            jax.ShapeDtypeStruct((vec_count, points), f32),
            jax.ShapeDtypeStruct((vec_count, points), bf16),
        ],
        grid_spec=pltpu.PrefetchScalarGridSpec(
            num_scalar_prefetch=2,
            grid=(steps,),
            in_specs=[
                pl.BlockSpec((vec_count, points), lambda i, *_: (0, 0)),
                pl.BlockSpec((vec_count, points), lambda i, *_: (0, 0)),
                pl.BlockSpec((group, leaf_size, leaf_size), lambda i, *_: (i, 0, 0)),
            ],
            out_specs=[
                pl.BlockSpec((vec_count, points), lambda i, *_: (0, 0)),
                pl.BlockSpec((vec_count, points), lambda i, *_: (0, 0)),
            ],
            scratch_shapes=[
                pltpu.VMEM((vec_count, 2 * points), bf16),
                pltpu.VMEM((vec_count, 2 * points), f32),
            ],
        ),
        compiler_params=params,
        name="near",
    )(near_rows, near_cols, vectors, following, near_tiles)
    spread, coef_send, term_send = lax.optimization_barrier((spread, coef_send, term_send))
    near_got = lax.ppermute(spread, "leaf", [(source, source + 1) for source in range(count - 1)])

    any_space = pl.BlockSpec(memory_space=pl.ANY)
    coef_got, term_got = pl.pallas_call(
        functools.partial(exchange_kernel, count, reach),
        out_shape=[packed, packed],
        in_specs=[any_space] * 2,
        out_specs=[any_space] * 2,
        scratch_shapes=[pltpu.SemaphoreType.DMA((reach,))] * 4,
        compiler_params=pltpu.CompilerParams(collective_id=0, has_side_effects=True),
        name="exchange",
    )(coef_send, term_send)

    return pl.pallas_call(
        functools.partial(downward_kernel, count, cap, offsets, leaf_count, leaf_size),
        out_shape=jax.ShapeDtypeStruct((vec_count, points), f32),
        in_specs=[SMEM] * 4 + [VMEM] * 12,
        out_specs=VMEM,
        scratch_shapes=[
            pltpu.VMEM((nodes, vec_count, rank), f32),
            pltpu.VMEM((2 * count, vec_count, rank), f32),
        ],
        compiler_params=params,
        name="downward",
    )(
        far_rows,
        far_cols,
        counts,
        ids,
        coefs,
        far_tiles,
        coef_got,
        term_got,
        roots,
        root_transfer,
        top_transfer.reshape(count // 2 - 1, 2 * rank, rank),
        top_couple,
        pairs,
        leaf_basis,
        near_own,
        near_got,
    )


def solution(mesh):
    in_specs = (
        P(None, "leaf"),
        P(None, "leaf"),
        P("leaf", None, None),
        P("leaf", None, None),
        P("leaf"),
        P("leaf"),
        P("leaf", None, None),
        P("leaf"),
        P("leaf"),
        P("leaf", None),
        P(),
        P(),
    )
    out_specs = P(None, "leaf")
    return jax.shard_map(body, mesh=mesh, in_specs=in_specs, out_specs=out_specs, check_vma=False)
```

time: 409 us -> 199 us (0.49)
  starting transfers between devices: 148 us -> 5.58 us
  Pallas kernels: 0 us -> 99.6 us
  blocking collectives: 0 us -> 82.6 us
  other arithmetic: 75.7 us -> 0.08 us
  matrix products: 68.4 us -> 0 us
  waiting for transfers between devices: 66 us -> 0.01 us
  local copies, waits for them, and re-layouts: 44.8 us -> 10.1 us
    ppermute x43 -> x2, starting transfers between devices: 148 us -> 5.58 us  [the longest x1 3.67 us: body(): lax.ppermute(vectors, 'leaf', [(source, source - 1) for source in range(1...]
    pallas_call x0 -> x5, Pallas kernels: none -> 99.6 us  [the longest x1 34.1 us: body(): pl.pallas_call(functools.partial(exchange_kernel, count, reach), out_shap...]
    scatter-add x3 -> x0, other arithmetic: 69.5 us -> none  [the longest x1 29.8 us: body(): far_nodes = jnp.zeros((node_count, vec_count, rank_size), jnp.float32).at...]
    dot_general x50 -> x0, matrix products: 68.4 us -> none  [the longest x1 12.1 us: body(): jnp.einsum('vnq,npq->vnp', jnp.take(joined, near_cols, axis=1), near_tile...]
    ppermute x43 -> x2, waiting for transfers between devices: 66 us -> 0.01 us  [the longest x1 0.01 us: body(): lax.ppermute(vectors, 'leaf', [(source, source - 1) for source in range(1...]
    all_gather x0 -> x1, blocking collectives: none -> 42.6 us  [body(): lax.all_gather(jnp.concatenate([root, root_transfer], axis=1), 'leaf')]
    unnamed x0 -> x1, blocking collectives: none -> 40 us
    gather x12 -> x0, local copies, waits for them, and re-layouts: 16.6 us -> none  [the longest x8 6.79 us: body(): jnp.take(node_coefs, got_ids, axis=0)]
  transfers between devices with their start and end apart: 43 -> 2, of which waited for: 14 -> 0; matrix products, arithmetic and copies ran while one was open for 40% -> 4% of each run, Pallas kernels for 0% -> 27%
where the time goes in v1:
time: 199 us; the launch traced here: 198 us
  Pallas kernels  99.6 us (50%)
  blocking collectives  82.6 us (42%)
  local copies, waits for them, and re-layouts  10.1 us (5%)
  starting transfers between devices  5.58 us (3%)
    all_gather x1, blocking collectives, body(): lax.all_gather(jnp.concatenate([root, root_transfer], axis=1), 'leaf')  42.6 us
    unnamed x1, blocking collectives  40 us
    pallas_call x1, Pallas kernels, body(): pl.pallas_call(functools.partial(exchange_kernel, count, reach), out_shap...  34.1 us
    pallas_call x1, Pallas kernels, body(): pl.pallas_call(functools.partial(downward_kernel, count, cap, offsets, le...  29.5 us
    pallas_call x1, Pallas kernels, body(): pl.pallas_call(functools.partial(pack_kernel, count, cap, offsets), out_s...  15.9 us
    pallas_call x1, Pallas kernels, body(): pl.pallas_call(functools.partial(near_kernel, group, steps, leaf_size, po...  15.9 us
    unnamed x13, local copies, waits for them, and re-layouts  7.1 us
    pallas_call x1, Pallas kernels, body(): pl.pallas_call(functools.partial(upward_kernel, leaf_count, leaf_size), o...  4.26 us
  transfers between devices with their start and end apart: 2, of which 0 were waited for; matrix products, arithmetic and copies ran while one was open for 4% of the time, Pallas kernels for 27%

profile of v1, /device:TPU:8, one launch (start us, length us, event | category | flops | bytes accessed | tf_op | source)
XLA Modules:
  0.0 198.1 jit_solution(16926122219895759018)
XLA Ops:
  0.0 3.7 %collective-permute-start = (bf16[64,8192]{1,0:T(8,128)(2,1)}, bf16[64,8192]{1,0:T(8,128)(2,1)S(1)}, u32[]{:S(2)}, u32[]{:S(2)}) collective-permute-start(bf16[64,8192]{1,0:T(8,128)(2,1)} %vec_ref.3), channel_id=1, source_target_pairs={{1,0},{2,1},{3,2},{4,3},{5,4},{6,5},{7,6},{8,7},{9,8},{10,9},{11,1... | collective-permute-start | bytes 3145736 | tf_op jit(solution)/shard_map/ppermute | solution.py:307
  3.7 2.3 %slice.6 = bf16[62,64,64]{2,1,0:T(8,128)(2,1)} slice(bf16[63,64,64]{2,1,0:T(8,128)(2,1)} %param.14), slice={[0:62], [0:64], [0:64]} | slice | bytes 1015808 | tf_op jit(solution)/shard_map/slice | solution.py:309
  5.9 4.8 %copy.14.tiles_ref = bf16[144,64,64]{2,1,0:T(8,128)(2,1)} copy(bf16[144,64,64]{0,2,1:T(8,128)(2,1)} %param.18) | data formatting | bytes 2359296 | tf_op args[6]
  10.8 0.0 copy-start.4
  10.8 4.3 %upward.1 = (bf16[63,64,64]{2,1,0:T(8,128)(2,1)}, bf16[64,64]{1,0:T(8,128)(2,1)}) custom-call(bf16[64,8192]{1,0:T(8,128)(2,1)} %vec_ref.3, bf16[64,8192]{1,0:T(8,128)(2,1)} %basis_ref.3, bf16[31,128,64]{2,1,0:T(8,128)(2,1)} %bitcast.6), custom_call_target="tpu_custom_call" | custom-call | tf_op jit(solution)/shard_map/upward/pallas_call | solution.py:312
  15.1 0.0 copy-done.4
  15.1 0.3 dynamic-update-slice
  15.3 40.0 %all-reduce.ids_ref = s32[4608]{0:T(1024)} all-reduce(s32[4608]{0:T(1024)S(1)} %dynamic-update-slice), channel_id=1, replica_groups=mesh['leaf'=32] {'leaf'}, use_global_device_ids=true, to_apply=%add | all-reduce | flops 4608 | bytes 36864
  55.3 15.9 %pack.1 = (bf16[8,8,64,128]{3,2,1,0:T(8,128)(2,1)}, bf16[8,8,64,128]{3,2,1,0:T(8,128)(2,1)}) custom-call(s32[144]{0:T(256)} %rows_ref.5, s32[9]{0:T(128)} %bitcast.10, s32[4608]{0:T(1024)} %all-reduce.ids_ref, bf16[63,64,64]{2,1,0:T(8,128)(2,1)} %get-tuple-element.16.coef_ref, bf16[144,64,64]{2,1,0:T(8,128)(2,1)} %copy.14.tiles_ref), custom_call_target="tpu_custom_call" | custom-call | tf_op jit(solution)/shard_map/pack/pallas_call | solution.py:326
  71.3 0.0 copy-start.3
  71.3 0.0 collective-permute-done.next_ref
  71.3 0.0 copy-start.1
  71.3 1.0 copy-done.1
  72.3 15.9 %near.1 = (f32[64,8192]{1,0:T(8,128)}, bf16[64,8192]{1,0:T(8,128)(2,1)}) custom-call(s32[96]{0:T(128)} %rows_ref.3, s32[96]{0:T(128)} %cols_ref.2, bf16[64,8192]{1,0:T(8,128)(2,1)} %vec_ref.3, bf16[64,8192]{1,0:T(8,128)(2,1)} %copy-done.1, bf16[96,256,256]{2,1,0:T(8,128)(2,1)} %tiles_ref.3), custom_call_target="tpu_custom_call" | custom-call | tf_op jit(solution)/shard_map/near/pallas_call | solution.py:337
  88.2 1.9 collective-permute-start.1
  90.1 0.7 slice_bitcast_fusion.transfer_ref
  90.8 0.0 copy-start.2
  90.8 0.0 copy-done.3
  90.8 0.1 pad_maximum_fusion
  90.9 42.6 %all-gather = bf16[2048,128]{1,0:T(8,128)(2,1)} all-gather(bf16[64,128]{1,0:T(8,128)(2,1)S(1)} %pad_maximum_fusion), channel_id=2, replica_groups=mesh['leaf'=32] {'leaf'}, dimensions={0}, use_global_device_ids=true | all-gather | bytes 540672 | tf_op jit(solution)/shard_map/all_gather | solution.py:323
  133.6 34.1 %exchange.1 = (bf16[8,8,64,128]{3,2,1,0:T(8,128)(2,1)}, bf16[8,8,64,128]{3,2,1,0:T(8,128)(2,1)}) custom-call(bf16[8,8,64,128]{3,2,1,0:T(8,128)(2,1)} %get-tuple-element.20.coef_in, bf16[8,8,64,128]{3,2,1,0:T(8,128)(2,1)} %get-tuple-element.21.term_in), custom_call_target="tpu_custom_call" | custom-call | tf_op jit(solution)/shard_map/exchange/pallas_call | solution.py:367
  167.6 0.0 collective-permute-done.1.got_ref
  167.6 0.0 copy-start
  167.6 0.0 copy-done.2
  167.7 1.0 copy-done
  168.6 29.5 %downward.1 = f32[64,8192]{1,0:T(8,128)} custom-call(s32[144]{0:T(256)} %rows_ref.5, s32[144]{0:T(256)} %cols_ref.3, s32[9]{0:T(128)} %bitcast.11, s32[4608]{0:T(1024)} %all-reduce.ids_ref, bf16[63,64,64]{2,1,0:T(8,128)(2,1)} %get-tuple-element.16.coef_ref, bf16[144,64,64]{2,1,0:T(8,128)(2,1)} %copy.14.tiles_ref, ...), custom_call_target="tpu_custom_call" | custom-call | tf_op jit(solution)/shard_map/downward/pallas_call | solution.py:377
  (1 shorter events, 0.0 us)
Async XLA Ops:
  0.0 71.3 %collective-permute-start = (bf16[64,8192]{1,0:T(8,128)(2,1)}, bf16[64,8192]{1,0:T(8,128)(2,1)S(1)}, u32[]{:S(2)}, u32[]{:S(2)}) collective-permute-start(bf16[64,8192]{1,0:T(8,128)(2,1)} %vec_ref.3), channel_id=1, source_target_pairs={{1,0},{2,1},{3,2},{4,3},{5,4},{6,5},{7,6},{8,7},{9,8},{10,9},{11,1... | collective-permute-start | bytes 3145736 | tf_op jit(solution)/shard_map/ppermute | solution.py:307
  10.8 4.3 %copy-start.4 = (s32[144]{0:T(256)S(1)}, s32[144]{0:T(256)}, u32[]{:S(2)}) copy-start(s32[144]{0:T(256)} %cols_ref.3) | copy-start | bytes 1732
  71.3 19.6 %copy-start.3 = (bf16[64,64]{1,0:T(8,128)(2,1)S(1)}, bf16[64,64]{1,0:T(8,128)(2,1)}, u32[]{:S(2)}) copy-start(bf16[64,64]{1,0:T(8,128)(2,1)} %get-tuple-element.24) | copy-start | bytes 24580
  71.3 1.0 copy-start.1
  88.2 79.4 %collective-permute-start.1 = (bf16[64,8192]{1,0:T(8,128)(2,1)}, bf16[64,8192]{1,0:T(8,128)(2,1)S(1)}, u32[]{:S(2)}, u32[]{:S(2)}) collective-permute-start(bf16[64,8192]{1,0:T(8,128)(2,1)} %get-tuple-element.26), channel_id=1, source_target_pairs={{0,1},{1,2},{2,3},{3,4},{4,5},{5,6},{6,7},{7,8},{8,9},{9,10},{10,1... | collective-permute-start | bytes 3145736 | tf_op jit(solution)/shard_map/ppermute | solution.py:364
  90.8 76.8 %copy-start.2 = (bf16[64,64]{1,0:T(8,128)(2,1)}, bf16[64,64]{1,0:T(8,128)(2,1)S(1)}, u32[]{:S(2)}) copy-start(bf16[64,64]{1,0:T(8,128)(2,1)S(1)} %slice_bitcast_fusion.transfer_ref) | copy-start | bytes 24580
  167.6 1.0 copy-start

commit v2 on v1

v2 whole, which is shorter than its diff:
```python
import functools

import jax
import jax.numpy as jnp
from jax import lax
from jax.experimental import pallas as pl
from jax.experimental.pallas import tpu as pltpu
from jax.sharding import PartitionSpec as P

f32 = jnp.float32
bf16 = jnp.bfloat16
highest = lax.Precision.HIGHEST
NT = (((1,), (1,)), ((), ()))
VMEM = pl.BlockSpec(memory_space=pltpu.VMEM)
SMEM = pl.BlockSpec(memory_space=pltpu.SMEM)
LIMIT = 56 * 1024 * 1024


def dot(a, b):
    return jnp.dot(a, b, preferred_element_type=f32)


def dot_nt(a, b):
    return lax.dot_general(a, b, NT, preferred_element_type=f32)


def dot_split(a, b):
    high = a.astype(bf16)
    low = (a - high.astype(f32)).astype(bf16)
    rows = a.shape[0]
    both = dot_nt(jnp.concatenate([high, low], axis=0), b)
    return both[:rows] + both[rows:]


def pack_rows(value):
    half = value.shape[0] // 2
    return jnp.concatenate([value[:half], value[half:]], axis=1)


def unpack_rows(value):
    half = value.shape[1] // 2
    return jnp.concatenate([value[:, :half], value[:, half:]], axis=0)


def child_pair(transfer_ref, node):
    rank = transfer_ref.shape[1]
    return transfer_ref[node : node + 2].reshape(2 * rank, rank)


def greet_all(me, count):
    barrier = pltpu.get_barrier_semaphore()

    @pl.loop(1, count)
    def _(turn):
        pl.semaphore_signal(
            barrier, inc=1, device_id=(lax.rem(me + turn, count),), device_id_type=pl.DeviceIdType.MESH
        )

    pl.semaphore_wait(barrier, count - 1)


def remote(source, target, send, recv, peer):
    return pltpu.make_async_remote_copy(
        src_ref=source,
        dst_ref=target,
        send_sem=send,
        recv_sem=recv,
        device_id=(peer,),
        device_id_type=pl.DeviceIdType.MESH,
    )


def upward_kernel(
    count,
    leaf_count,
    leaf_size,
    reach,
    vec_ref,
    basis_ref,
    transfer_ref,
    cols_ref,
    coef_ref,
    root_ref,
    ids_ref,
    lifts_ref,
    lift_buf,
    id_send,
    id_recv,
    lift_send,
    lift_recv,
    own_sem,
):
    me = lax.axis_index("leaf")
    nodes = transfer_ref.shape[0]
    lift_buf[...] = pack_rows(transfer_ref[nodes - 1])
    greet_all(me, count)

    def id_copy(step):
        return remote(
            cols_ref, ids_ref.at[step - 1], id_send.at[step - 1], id_recv.at[step - 1], me + step
        )

    def lift_copy(turn):
        peer = lax.rem(me + turn, count)
        return remote(lift_buf, lifts_ref.at[me], lift_send.at[turn], lift_recv.at[turn], peer)

    for step in range(1, reach + 1):

        @pl.when(me + step < count)
        def _(step=step):
            id_copy(step).start()

    own = pltpu.make_async_copy(lift_buf, lifts_ref.at[me], own_sem)
    own.start()

    @pl.loop(1, count)
    def _(turn):
        lift_copy(turn).start()

    current = []
    for leaf in range(leaf_count):
        span = slice(leaf * leaf_size, (leaf + 1) * leaf_size)
        current.append(dot_nt(vec_ref[:, span], basis_ref[:, span]).astype(bf16))
    offset = 0
    while True:
        for spot, value in enumerate(current):
            coef_ref[offset + spot] = value
        if len(current) == 1:
            break
        parents = []
        for pair in range(len(current) // 2):
            joined = jnp.concatenate([current[2 * pair], current[2 * pair + 1]], axis=1)
            parents.append(dot(joined, child_pair(transfer_ref, offset + 2 * pair)).astype(bf16))
        offset += len(current)
        current = parents
    root_ref[...] = pack_rows(current[0])
    own.wait()

    @pl.loop(1, count)
    def _(turn):
        lift_copy(turn).wait()

    for step in range(1, reach + 1):

        @pl.when(me + step < count)
        def _(step=step):
            id_copy(step).wait_send()

        @pl.when(me - step >= 0)
        def _(step=step):
            id_copy(step).wait_recv()


def exchange_kernel(
    count,
    cap,
    offsets,
    rows_ref,
    counts_ref,
    ids_ref,
    coef_ref,
    tiles_ref,
    root_ref,
    coef_got,
    term_got,
    roots_ref,
    coef_buf,
    term_buf,
    coef_send,
    coef_recv,
    term_send,
    term_recv,
    root_send,
    root_recv,
    own_sem,
):
    me = lax.axis_index("leaf")
    reach = offsets - 1
    greet_all(me, count)

    def root_copy(turn):
        peer = lax.rem(me + turn, count)
        return remote(root_ref, roots_ref.at[me], root_send.at[turn], root_recv.at[turn], peer)

    def back(step):
        at = step - 1
        return remote(coef_buf.at[at], coef_got.at[at], coef_send.at[at], coef_recv.at[at], me - step)

    def ahead(step):
        at = step - 1
        return remote(term_buf.at[at], term_got.at[at], term_send.at[at], term_recv.at[at], me + step)

    own = pltpu.make_async_copy(root_ref, roots_ref.at[me], own_sem)
    own.start()

    for step in range(reach, 0, -1):

        @pl.when(me - step >= 0)
        def _(step=step):
            for pair in range(cap // 2):
                slot = step * cap + 2 * pair
                values = [coef_ref[ids_ref[step - 1, 0, slot + half]] for half in range(2)]
                coef_buf[step - 1, pair] = jnp.concatenate(values, axis=1)
            back(step).start()

        @pl.when(me + step < count)
        def _(step=step):
            for pair in range(cap // 2):
                terms = []
                for half in range(2):
                    spot = 2 * pair + half
                    slot = step * cap + spot
                    term = dot(coef_ref[rows_ref[slot]], tiles_ref[slot])
                    terms.append(jnp.where(spot < counts_ref[step], term, 0.0).astype(bf16))
                term_buf[step - 1, pair] = jnp.concatenate(terms, axis=1)
            ahead(step).start()

    @pl.loop(1, count)
    def _(turn):
        root_copy(turn).start()

    own.wait()

    @pl.loop(1, count)
    def _(turn):
        root_copy(turn).wait()

    for step in range(1, reach + 1):

        @pl.when(me - step >= 0)
        def _(step=step):
            back(step).wait_send()
            ahead(step).wait_recv()

        @pl.when(me + step < count)
        def _(step=step):
            ahead(step).wait_send()
            back(step).wait_recv()


def near_kernel(
    group, steps, leaf_size, points, rows_ref, cols_ref, vec_ref, next_ref, tiles_ref, own_ref, spread_ref, joined, total
):
    step = pl.program_id(0)

    @pl.when(step == 0)
    def _():
        joined[:, :points] = vec_ref[...]
        joined[:, points:] = next_ref[...]
        total[...] = jnp.zeros_like(total)

    for spot in range(group):
        tile = tiles_ref[spot]
        row = pl.ds(pl.multiple_of(rows_ref[step * group + spot] * leaf_size, leaf_size), leaf_size)
        col = pl.ds(pl.multiple_of(cols_ref[step * group + spot] * leaf_size, leaf_size), leaf_size)
        to_row = dot_nt(joined[:, col], tile)
        to_col = dot(joined[:, row], tile)
        total[:, row] += to_row
        total[:, col] += to_col

    @pl.when(step == steps - 1)
    def _():
        own_ref[...] = total[:, :points]
        spread_ref[...] = total[:, points:].astype(bf16)


def downward_kernel(
    count,
    cap,
    offsets,
    leaf_count,
    leaf_size,
    chunks,
    rows_ref,
    cols_ref,
    counts_ref,
    ids_ref,
    coef_ref,
    tiles_ref,
    coef_got,
    term_got,
    roots_ref,
    lifts_ref,
    transfer_ref,
    top_hbm,
    couple_hbm,
    basis_hbm,
    own_hbm,
    got_hbm,
    out_hbm,
    far,
    level,
    top_ref,
    couple_ref,
    basis_ref,
    own_ref,
    got_ref,
    load_sem,
    out_sem,
):
    me = lax.axis_index("leaf")
    rank = coef_ref.shape[1]
    late = [(top_hbm, top_ref), (couple_hbm, couple_ref), (basis_hbm, basis_ref)]
    late += [(own_hbm, own_ref), (got_hbm, got_ref)]
    loads = [pltpu.make_async_copy(a, b, load_sem.at[i]) for i, (a, b) in enumerate(late)]
    for load in loads:
        load.start()
    far[...] = jnp.zeros_like(far)

    to_row = []
    to_col = []
    for spot in range(cap):
        tile = tiles_ref[spot]
        used = spot < counts_ref[0]
        to_row.append(jnp.where(used, dot_nt(coef_ref[cols_ref[spot]], tile), 0.0))
        to_col.append(jnp.where(used, dot(coef_ref[rows_ref[spot]], tile), 0.0))
    for spot in range(cap):
        far[rows_ref[spot]] += to_row[spot]
        far[cols_ref[spot]] += to_col[spot]

    for step in range(1, offsets):

        @pl.when(me + step < count)
        def _(step=step):
            terms = []
            for spot in range(cap):
                half = spot % 2
                values = coef_got[step - 1, spot // 2][:, half * rank : (half + 1) * rank]
                term = dot_nt(values, tiles_ref[step * cap + spot])
                terms.append(jnp.where(spot < counts_ref[step], term, 0.0))
            for spot in range(cap):
                far[rows_ref[step * cap + spot]] += terms[spot]

        @pl.when(me - step >= 0)
        def _(step=step):
            for spot in range(cap):
                half = spot % 2
                values = term_got[step - 1, spot // 2][:, half * rank : (half + 1) * rank]
                far[ids_ref[step - 1, 0, step * cap + spot]] += values.astype(f32)

    loads[0].wait()
    loads[1].wait()
    for node in range(count // 2):
        left = unpack_rows(roots_ref[2 * node])
        right = unpack_rows(roots_ref[2 * node + 1])
        joined = jnp.concatenate([left, right], axis=1)
        lift = [unpack_rows(lifts_ref[2 * node + half]) for half in range(2)]
        level[count // 2 + node] = dot(joined, jnp.concatenate(lift, axis=0))
        level[count + 2 * node] = left.astype(f32)
        level[count + 2 * node + 1] = right.astype(f32)
    for node in range(count // 2 - 1, 1, -1):
        joined = jnp.concatenate([level[2 * node], level[2 * node + 1]], axis=1)
        level[node] = jnp.dot(joined, top_ref[node - 1], precision=highest, preferred_element_type=f32)
    heights = count.bit_length() - 1
    heap = count + me
    going = None
    for height in range(heights - 1, -1, -1):
        node = heap >> height
        other = level[node ^ 1]
        tile = couple_ref[(node >> 1) - 1]
        turned = jnp.where(node % 2 == 0, tile.T, tile)
        term = jnp.dot(other, turned, precision=highest, preferred_element_type=f32)
        if going is None:
            going = term
        elif height == 0:
            going = term + dot_split(going, transfer_ref[transfer_ref.shape[0] - 1])
        else:
            lift = transfer_of(top_ref, node - 2, rank)
            going = term + lax.dot_general(going, lift, NT, precision=highest, preferred_element_type=f32)

    offset = far.shape[0] - 1
    current = [far[offset] + going]
    while len(current) < leaf_count:
        offset -= 2 * len(current)
        children = []
        for spot, value in enumerate(current):
            both = dot_split(value, child_pair(transfer_ref, offset + 2 * spot))
            children.append(far[offset + 2 * spot] + both[:, :rank])
            children.append(far[offset + 2 * spot + 1] + both[:, rank:])
        current = children
    for load in loads[2:]:
        load.wait()
    width = leaf_count * leaf_size // chunks
    stores = []
    for leaf, value in enumerate(current):
        span = slice(leaf * leaf_size, (leaf + 1) * leaf_size)
        term = dot(value.astype(bf16), basis_ref[:, span])
        own_ref[:, span] = own_ref[:, span] + got_ref[:, span].astype(f32) + term
        if (leaf + 1) * leaf_size % width == 0:
            part = pl.ds(len(stores) * width, width)
            store = pltpu.make_async_copy(own_ref.at[:, part], out_hbm.at[:, part], out_sem.at[len(stores)])
            store.start()
            stores.append(store)
    for store in stores:
        store.wait()


def transfer_of(top_ref, index, rank):
    start = pl.multiple_of((index % 2) * rank, rank)
    return top_ref[index // 2, pl.ds(start, rank), :]


def body(
    vectors,
    leaf_basis,
    local_transfer,
    near_tiles,
    near_rows,
    near_cols,
    far_tiles,
    far_rows,
    far_cols,
    far_counts,
    top_transfer,
    top_couple,
):
    vec_count, points = vectors.shape
    rank = leaf_basis.shape[0]
    near_count, leaf_size, _ = near_tiles.shape
    leaf_count = points // leaf_size
    nodes = local_transfer.shape[0]
    count = lax.axis_size("leaf")
    slots = far_tiles.shape[0]
    offsets = far_counts.shape[1]
    reach = offsets - 1
    cap = slots // offsets
    counts = far_counts[0]
    params = pltpu.CompilerParams(vmem_limit_bytes=LIMIT)

    following = lax.ppermute(vectors, "leaf", [(source, source - 1) for source in range(1, count)])
    any_space = pl.BlockSpec(memory_space=pl.ANY)
    dma = pltpu.SemaphoreType.DMA
    half_rows = jax.ShapeDtypeStruct((count, rank // 2, 2 * rank), bf16)

    coefs, root, ids, lifts = pl.pallas_call(
        functools.partial(upward_kernel, count, leaf_count, leaf_size, reach),
        out_shape=[
            jax.ShapeDtypeStruct((nodes, vec_count, rank), bf16),
            jax.ShapeDtypeStruct((vec_count // 2, 2 * rank), bf16),
            jax.ShapeDtypeStruct((reach, 1, slots), jnp.int32),
            half_rows,
        ],
        in_specs=[VMEM] * 3 + [any_space],
        out_specs=[VMEM] * 2 + [any_space] * 2,
        scratch_shapes=[pltpu.VMEM((rank // 2, 2 * rank), bf16)]
        + [dma((reach,))] * 2
        + [dma((count,))] * 2
        + [dma(())],
        compiler_params=pltpu.CompilerParams(
            collective_id=0, has_side_effects=True, vmem_limit_bytes=LIMIT
        ),
        name="upward",
    )(vectors, leaf_basis, local_transfer, far_cols.reshape(1, slots))

    group = 8
    steps = near_count // group
    near_own, spread = pl.pallas_call(
        functools.partial(near_kernel, group, steps, leaf_size, points),
        out_shape=[
            jax.ShapeDtypeStruct((vec_count, points), f32),
            jax.ShapeDtypeStruct((vec_count, points), bf16),
        ],
        grid_spec=pltpu.PrefetchScalarGridSpec(
            num_scalar_prefetch=2,
            grid=(steps,),
            in_specs=[
                pl.BlockSpec((vec_count, points), lambda i, *_: (0, 0)),
                pl.BlockSpec((vec_count, points), lambda i, *_: (0, 0)),
                pl.BlockSpec((group, leaf_size, leaf_size), lambda i, *_: (i, 0, 0)),
            ],
            out_specs=[
                pl.BlockSpec((vec_count, points), lambda i, *_: (0, 0)),
                pl.BlockSpec((vec_count, points), lambda i, *_: (0, 0)),
            ],
            scratch_shapes=[
                pltpu.VMEM((vec_count, 2 * points), bf16),
                pltpu.VMEM((vec_count, 2 * points), f32),
            ],
        ),
        compiler_params=params,
        name="near",
    )(near_rows, near_cols, vectors, following, near_tiles)
    spread, coefs = lax.optimization_barrier((spread, coefs))
    near_got = lax.ppermute(spread, "leaf", [(source, source + 1) for source in range(count - 1)])

    packed = (reach, cap // 2, vec_count, 2 * rank)
    coef_got, term_got, roots = pl.pallas_call(
        functools.partial(exchange_kernel, count, cap, offsets),
        out_shape=[
            jax.ShapeDtypeStruct(packed, bf16),
            jax.ShapeDtypeStruct(packed, bf16),
            jax.ShapeDtypeStruct((count, vec_count // 2, 2 * rank), bf16),
        ],
        in_specs=[SMEM] * 3 + [VMEM] * 3,
        out_specs=[any_space] * 3,
        scratch_shapes=[pltpu.VMEM(packed, bf16)] * 2
        + [dma((reach,))] * 4
        + [dma((count,))] * 2
        + [dma(())],
        compiler_params=pltpu.CompilerParams(
            collective_id=1, has_side_effects=True, vmem_limit_bytes=LIMIT
        ),
        name="exchange",
    )(far_rows, counts, ids, coefs, far_tiles, root)

    chunks = 4
    top_pairs = top_transfer.reshape(count // 2 - 1, 2 * rank, rank)
    return pl.pallas_call(
        functools.partial(downward_kernel, count, cap, offsets, leaf_count, leaf_size, chunks),
        out_shape=jax.ShapeDtypeStruct((vec_count, points), f32),
        in_specs=[SMEM] * 4 + [VMEM] * 7 + [any_space] * 5,
        out_specs=any_space,
        scratch_shapes=[
            pltpu.VMEM((nodes, vec_count, rank), f32),
            pltpu.VMEM((2 * count, vec_count, rank), f32),
            pltpu.VMEM(top_pairs.shape, f32),
            pltpu.VMEM(top_couple.shape, f32),
            pltpu.VMEM(leaf_basis.shape, bf16),
            pltpu.VMEM(near_own.shape, f32),
            pltpu.VMEM(near_got.shape, bf16),
            dma((5,)),
            dma((chunks,)),
        ],
        compiler_params=params,
        name="downward",
    )(
        far_rows,
        far_cols,
        counts,
        ids,
        coefs,
        far_tiles,
        coef_got,
        term_got,
        roots,
        lifts,
        local_transfer,
        top_pairs,
        top_couple,
        leaf_basis,
        near_own,
        near_got,
    )


def solution(mesh):
    in_specs = (
        P(None, "leaf"),
        P(None, "leaf"),
        P("leaf", None, None),
        P("leaf", None, None),
        P("leaf"),
        P("leaf"),
        P("leaf", None, None),
        P("leaf"),
        P("leaf"),
        P("leaf", None),
        P(),
        P(),
    )
    out_specs = P(None, "leaf")
    return jax.shard_map(body, mesh=mesh, in_specs=in_specs, out_specs=out_specs, check_vma=False)
```

time: 199 us -> 103 us (0.52)
  blocking collectives: 82.6 us -> 0 us
  Pallas kernels: 99.6 us -> 90.2 us
  local copies, waits for them, and re-layouts: 10.1 us -> 5.3 us
    all_gather x1 -> x0, blocking collectives: 42.6 us -> none  [body(): lax.all_gather(jnp.concatenate([root, root_transfer], axis=1), 'leaf')]
    unnamed x1 -> x0, blocking collectives: 40 us -> none
    pallas_call x1, Pallas kernels: 29.5 us -> 12.4 us  [body(): pl.pallas_call(functools.partial(downward_kernel, count, cap, offsets, le...]
    pallas_call x3 -> x2, Pallas kernels: 54.3 us -> 62 us  [the longest x1 40.6 us: body(): pl.pallas_call(functools.partial(exchange_kernel, count, cap, offsets), o...]
    slice x1 -> x0, local copies, waits for them, and re-layouts: 2.26 us -> none  [body(): pairs = local_transfer[:nodes - 1].reshape(nodes // 2, 2 * rank, rank)]
    unnamed x13 -> x7, local copies, waits for them, and re-layouts: 7.1 us -> 5.3 us
  transfers between devices with their start and end apart: 2 -> 2, of which waited for: 0 -> 0; matrix products, arithmetic and copies ran while one was open for 4% -> 3% of each run, Pallas kernels for 27% -> 61%
where the time goes in v2:
time: 103 us; the launch traced here: 101 us
  Pallas kernels  90.2 us (88%)
  starting transfers between devices  5.59 us (5%)
  local copies, waits for them, and re-layouts  5.3 us (5%)
    pallas_call x1, Pallas kernels, body(): pl.pallas_call(functools.partial(exchange_kernel, count, cap, offsets), o...  40.6 us
    pallas_call x1, Pallas kernels, body(): pl.pallas_call(functools.partial(upward_kernel, count, leaf_count, leaf_s...  21.3 us
    pallas_call x1, Pallas kernels, body(): pl.pallas_call(functools.partial(near_kernel, group, steps, leaf_size, po...  15.9 us
    pallas_call x1, Pallas kernels, body(): pl.pallas_call(functools.partial(downward_kernel, count, cap, offsets, le...  12.4 us
    unnamed x7, local copies, waits for them, and re-layouts  5.3 us
    ppermute x1, starting transfers between devices, body(): lax.ppermute(vectors, 'leaf', [(source, source - 1) for source in range(1...  3.67 us
  transfers between devices with their start and end apart: 2, of which 0 were waited for; matrix products, arithmetic and copies ran while one was open for 3% of the time, Pallas kernels for 61%

profile of v2, /device:TPU:8, one launch (start us, length us, event | category | flops | bytes accessed | tf_op | source)
XLA Modules:
  0.0 101.2 jit_solution(9321845942973308525)
XLA Ops:
  0.0 3.7 %collective-permute-start = (bf16[64,8192]{1,0:T(8,128)(2,1)}, bf16[64,8192]{1,0:T(8,128)(2,1)S(1)}, u32[]{:S(2)}, u32[]{:S(2)}) collective-permute-start(bf16[64,8192]{1,0:T(8,128)(2,1)} %vec_ref.3), channel_id=1, source_target_pairs={{1,0},{2,1},{3,2},{4,3},{5,4},{6,5},{7,6},{8,7},{9,8},{10,9},{11,1... | collective-permute-start | bytes 3145736 | tf_op jit(solution)/shard_map/ppermute | solution.py:430
  3.7 21.3 %upward.1 = (bf16[63,64,64]{2,1,0:T(8,128)(2,1)}, bf16[32,128]{1,0:T(8,128)(2,1)}, s32[8,1,144]{2,1,0:T(1,128)}, bf16[32,32,128]{2,1,0:T(8,128)(2,1)}) custom-call(bf16[64,8192]{1,0:T(8,128)(2,1)} %vec_ref.3, bf16[64,8192]{1,0:T(8,128)(2,1)} %basis_hbm.1, bf16[63,64,64]{2,1,0:T(8,128)(2,1)} %transfer_ref.3, s32[1,144]{1,0:T(1,128)} %bitcast.4), custom_call_target="tpu_custom_call" | custom-call | tf_op jit(solution)/shard_map/upward/pallas_call | solution.py:435
  25.0 0.0 copy-start
  25.0 0.0 collective-permute-done.next_ref
  25.0 0.0 copy-start.2
  25.0 1.0 copy-done.2
  26.0 15.9 %near.1 = (f32[64,8192]{1,0:T(8,128)}, bf16[64,8192]{1,0:T(8,128)(2,1)}) custom-call(s32[96]{0:T(128)} %rows_ref.3, s32[96]{0:T(128)} %cols_ref.2, bf16[64,8192]{1,0:T(8,128)(2,1)} %vec_ref.3, bf16[64,8192]{1,0:T(8,128)(2,1)} %copy-done.2, bf16[96,256,256]{2,1,0:T(8,128)(2,1)} %tiles_ref.3), custom_call_target="tpu_custom_call" | custom-call | tf_op jit(solution)/shard_map/near/pallas_call | solution.py:457
  41.9 1.9 %collective-permute-start.1 = (bf16[64,8192]{1,0:T(8,128)(2,1)}, bf16[64,8192]{1,0:T(8,128)(2,1)S(1)}, u32[]{:S(2)}, u32[]{:S(2)}) collective-permute-start(bf16[64,8192]{1,0:T(8,128)(2,1)} %get-tuple-element.26), channel_id=1, source_target_pairs={{0,1},{1,2},{2,3},{3,4},{4,5},{5,6},{6,7},{7,8},{8,9},{9,10},{10,1... | collective-permute-start | bytes 3145736 | tf_op jit(solution)/shard_map/ppermute | solution.py:484
  43.8 0.0 copy-done
  43.8 3.4 %copy.14.tiles_ref = bf16[144,64,64]{2,1,0:T(8,128)(2,1)} copy(bf16[144,64,64]{0,2,1:T(8,128)(2,1)S(1)} %copy-done) | data formatting | bytes 2359296 | tf_op args[6]
  47.2 40.6 %exchange.1 = (bf16[8,8,64,128]{3,2,1,0:T(8,128)(2,1)}, bf16[8,8,64,128]{3,2,1,0:T(8,128)(2,1)}, bf16[32,32,128]{2,1,0:T(8,128)(2,1)}) custom-call(s32[144]{0:T(256)} %rows_ref.5, s32[9]{0:T(128)} %bitcast.5, s32[8,1,144]{2,1,0:T(1,128)} %get-tuple-element.16.ids_ref, bf16[63,64,64]{2,1,0:T(8,128)(2,1)} %get-tuple-element.19.coef_ref, ...), custom_call_target="tpu_custom_call" | custom-call | tf_op jit(solution)/shard_map/exchange/pallas_call | solution.py:487
  87.9 0.0 collective-permute-done.1.got_hbm
  87.9 0.0 copy-start.1
  87.9 1.0 copy-done.1
  88.8 12.4 %downward.1 = f32[64,8192]{1,0:T(8,128)} custom-call(s32[144]{0:T(256)} %rows_ref.5, s32[144]{0:T(256)} %cols_ref.3, s32[9]{0:T(128)} %bitcast.6, s32[8,1,144]{2,1,0:T(1,128)} %get-tuple-element.16.ids_ref, bf16[63,64,64]{2,1,0:T(8,128)(2,1)} %get-tuple-element.19.coef_ref, bf16[144,64,64]{2,1,0:T(8,128)(2,1)} %copy.14.tiles_ref, ...), custom_call_target="tpu_custom_call" | custom-call | tf_op jit(solution)/shard_map/downward/pallas_call | solution.py:508
Async XLA Ops:
  0.0 25.0 %collective-permute-start = (bf16[64,8192]{1,0:T(8,128)(2,1)}, bf16[64,8192]{1,0:T(8,128)(2,1)S(1)}, u32[]{:S(2)}, u32[]{:S(2)}) collective-permute-start(bf16[64,8192]{1,0:T(8,128)(2,1)} %vec_ref.3), channel_id=1, source_target_pairs={{1,0},{2,1},{3,2},{4,3},{5,4},{6,5},{7,6},{8,7},{9,8},{10,9},{11,1... | collective-permute-start | bytes 3145736 | tf_op jit(solution)/shard_map/ppermute | solution.py:430
  25.0 18.8 %copy-start = (bf16[144,64,64]{0,2,1:T(8,128)(2,1)S(1)}, bf16[144,64,64]{0,2,1:T(8,128)(2,1)}, u32[]{:S(2)}) copy-start(bf16[144,64,64]{0,2,1:T(8,128)(2,1)} %param.18) | copy-start | bytes 3538948
  25.0 1.0 copy-start.2
  41.9 46.0 %collective-permute-start.1 = (bf16[64,8192]{1,0:T(8,128)(2,1)}, bf16[64,8192]{1,0:T(8,128)(2,1)S(1)}, u32[]{:S(2)}, u32[]{:S(2)}) collective-permute-start(bf16[64,8192]{1,0:T(8,128)(2,1)} %get-tuple-element.26), channel_id=1, source_target_pairs={{0,1},{1,2},{2,3},{3,4},{4,5},{5,6},{6,7},{7,8},{8,9},{9,10},{10,1... | collective-permute-start | bytes 3145736 | tf_op jit(solution)/shard_map/ppermute | solution.py:484
  87.9 1.0 copy-start.1

commit v3 on v2

--- a/solution.py
+++ b/solution.py
@@ -32,31 +32,37 @@
     return both[:rows] + both[rows:]
 
 
-def pack_rows(value):
-    half = value.shape[0] // 2
-    return jnp.concatenate([value[:half], value[half:]], axis=1)
-
-
-def unpack_rows(value):
-    half = value.shape[1] // 2
-    return jnp.concatenate([value[:, :half], value[:, half:]], axis=0)
-
-
 def child_pair(transfer_ref, node):
     rank = transfer_ref.shape[1]
     return transfer_ref[node : node + 2].reshape(2 * rank, rank)
 
 
-def greet_all(me, count):
+def partner_of(me, height):
+    mask = 2**height
+    return me + mask - 2 * mask * ((me // mask) % 2)
+
+
+def greet(me, count, reach, heights):
     barrier = pltpu.get_barrier_semaphore()
 
-    @pl.loop(1, count)
-    def _(turn):
+    def signal(peer):
         pl.semaphore_signal(
-            barrier, inc=1, device_id=(lax.rem(me + turn, count),), device_id_type=pl.DeviceIdType.MESH
+            barrier, inc=1, device_id=(peer,), device_id_type=pl.DeviceIdType.MESH
         )
 
-    pl.semaphore_wait(barrier, count - 1)
+    for step in range(1, reach + 1):
+
+        @pl.when(me - step >= 0)
+        def _(step=step):
+            signal(me - step)
+
+        @pl.when(me + step < count)
+        def _(step=step):
+            signal(me + step)
+
+    for height in range(heights):
+        signal(partner_of(me, height))
+    pl.semaphore_wait(barrier, jnp.minimum(me, reach) + jnp.minimum(count - 1 - me, reach) + heights)
 
 
 def remote(source, target, send, recv, peer):
@@ -82,40 +88,23 @@
     coef_ref,
     root_ref,
     ids_ref,
-    lifts_ref,
-    lift_buf,
     id_send,
     id_recv,
-    lift_send,
-    lift_recv,
-    own_sem,
 ):
     me = lax.axis_index("leaf")
     nodes = transfer_ref.shape[0]
-    lift_buf[...] = pack_rows(transfer_ref[nodes - 1])
-    greet_all(me, count)
+    greet(me, count, reach, 0)
 
     def id_copy(step):
         return remote(
             cols_ref, ids_ref.at[step - 1], id_send.at[step - 1], id_recv.at[step - 1], me + step
         )
 
-    def lift_copy(turn):
-        peer = lax.rem(me + turn, count)
-        return remote(lift_buf, lifts_ref.at[me], lift_send.at[turn], lift_recv.at[turn], peer)
-
     for step in range(1, reach + 1):
 
         @pl.when(me + step < count)
         def _(step=step):
             id_copy(step).start()
-
-    own = pltpu.make_async_copy(lift_buf, lifts_ref.at[me], own_sem)
-    own.start()
-
-    @pl.loop(1, count)
-    def _(turn):
-        lift_copy(turn).start()
 
     current = []
     for leaf in range(leaf_count):
@@ -133,12 +122,8 @@
             parents.append(dot(joined, child_pair(transfer_ref, offset + 2 * pair)).astype(bf16))
         offset += len(current)
         current = parents
-    root_ref[...] = pack_rows(current[0])
-    own.wait()
-
-    @pl.loop(1, count)
-    def _(turn):
-        lift_copy(turn).wait()
+    lift = dot(current[0], transfer_ref[nodes - 1])
+    root_ref[...] = jnp.concatenate([current[0].astype(f32), lift], axis=1)
 
     for step in range(1, reach + 1):
 
@@ -161,26 +146,58 @@
     coef_ref,
     tiles_ref,
     root_ref,
+    top_hbm,
     coef_got,
     term_got,
-    roots_ref,
+    other_ref,
     coef_buf,
     term_buf,
+    top_buf,
+    own_buf,
+    other_buf,
     coef_send,
     coef_recv,
     term_send,
     term_recv,
-    root_send,
-    root_recv,
-    own_sem,
+    own_send,
+    own_recv,
+    top_sem,
 ):
     me = lax.axis_index("leaf")
     reach = offsets - 1
-    greet_all(me, count)
-
-    def root_copy(turn):
-        peer = lax.rem(me + turn, count)
-        return remote(root_ref, roots_ref.at[me], root_send.at[turn], root_recv.at[turn], peer)
+    heights = count.bit_length() - 1
+    rank = coef_ref.shape[2]
+    lifts = [
+        pltpu.make_async_copy(
+            top_hbm.at[(count + me) // 2 ** (height + 1) - 2], top_buf.at[height], top_sem.at[height]
+        )
+        for height in range(heights - 1)
+    ]
+    for lift in lifts:
+        lift.start()
+    own_buf[0] = root_ref[...]
+    greet(me, count, reach, heights)
+    for lift in lifts:
+        lift.wait()
+
+    def swap(height):
+        return remote(
+            own_buf.at[height],
+            other_buf.at[height],
+            own_send.at[height],
+            own_recv.at[height],
+            partner_of(me, height),
+        )
+
+    def climb(height):
+        swap(height).wait()
+        other = other_buf[height]
+        other_ref[height] = other[:, :rank]
+        if height + 1 < heights:
+            coef = own_buf[height][:, rank:] + other[:, rank:]
+            lift = jnp.dot(coef, top_buf[height], precision=highest, preferred_element_type=f32)
+            own_buf[height + 1] = jnp.concatenate([coef, lift], axis=1)
+            swap(height + 1).start()
 
     def back(step):
         at = step - 1
@@ -190,9 +207,8 @@
         at = step - 1
         return remote(term_buf.at[at], term_got.at[at], term_send.at[at], term_recv.at[at], me + step)
 
-    own = pltpu.make_async_copy(root_ref, roots_ref.at[me], own_sem)
-    own.start()
-
+    swap(0).start()
+    height = 0
     for step in range(reach, 0, -1):
 
         @pl.when(me - step >= 0)
@@ -215,15 +231,12 @@
                 term_buf[step - 1, pair] = jnp.concatenate(terms, axis=1)
             ahead(step).start()
 
-    @pl.loop(1, count)
-    def _(turn):
-        root_copy(turn).start()
-
-    own.wait()
-
-    @pl.loop(1, count)
-    def _(turn):
-        root_copy(turn).wait()
+        if height < heights:
+            climb(height)
+            height += 1
+
+    for later in range(height, heights):
+        climb(later)
 
     for step in range(1, reach + 1):
 
@@ -279,8 +292,7 @@
     tiles_ref,
     coef_got,
     term_got,
-    roots_ref,
-    lifts_ref,
+    others_ref,
     transfer_ref,
     top_hbm,
     couple_hbm,
@@ -289,7 +301,6 @@
     got_hbm,
     out_hbm,
     far,
-    level,
     top_ref,
     couple_ref,
     basis_ref,
@@ -340,23 +351,12 @@
 
     loads[0].wait()
     loads[1].wait()
-    for node in range(count // 2):
-        left = unpack_rows(roots_ref[2 * node])
-        right = unpack_rows(roots_ref[2 * node + 1])
-        joined = jnp.concatenate([left, right], axis=1)
-        lift = [unpack_rows(lifts_ref[2 * node + half]) for half in range(2)]
-        level[count // 2 + node] = dot(joined, jnp.concatenate(lift, axis=0))
-        level[count + 2 * node] = left.astype(f32)
-        level[count + 2 * node + 1] = right.astype(f32)
-    for node in range(count // 2 - 1, 1, -1):
-        joined = jnp.concatenate([level[2 * node], level[2 * node + 1]], axis=1)
-        level[node] = jnp.dot(joined, top_ref[node - 1], precision=highest, preferred_element_type=f32)
     heights = count.bit_length() - 1
     heap = count + me
     going = None
     for height in range(heights - 1, -1, -1):
         node = heap >> height
-        other = level[node ^ 1]
+        other = others_ref[height]
         tile = couple_ref[(node >> 1) - 1]
         turned = jnp.where(node % 2 == 0, tile.T, tile)
         term = jnp.dot(other, turned, precision=highest, preferred_element_type=f32)
@@ -365,7 +365,7 @@
         elif height == 0:
             going = term + dot_split(going, transfer_ref[transfer_ref.shape[0] - 1])
         else:
-            lift = transfer_of(top_ref, node - 2, rank)
+            lift = top_ref[node - 2]
             going = term + lax.dot_general(going, lift, NT, precision=highest, preferred_element_type=f32)
 
     offset = far.shape[0] - 1
@@ -393,11 +393,6 @@
             stores.append(store)
     for store in stores:
         store.wait()
-
-
-def transfer_of(top_ref, index, rank):
-    start = pl.multiple_of((index % 2) * rank, rank)
-    return top_ref[index // 2, pl.ds(start, rank), :]
 
 
 def body(
@@ -430,22 +425,18 @@
     following = lax.ppermute(vectors, "leaf", [(source, source - 1) for source in range(1, count)])
     any_space = pl.BlockSpec(memory_space=pl.ANY)
     dma = pltpu.SemaphoreType.DMA
-    half_rows = jax.ShapeDtypeStruct((count, rank // 2, 2 * rank), bf16)
-
-    coefs, root, ids, lifts = pl.pallas_call(
+    heights = count.bit_length() - 1
+
+    coefs, root, ids = pl.pallas_call(
         functools.partial(upward_kernel, count, leaf_count, leaf_size, reach),
         out_shape=[
             jax.ShapeDtypeStruct((nodes, vec_count, rank), bf16),
-            jax.ShapeDtypeStruct((vec_count // 2, 2 * rank), bf16),
+            jax.ShapeDtypeStruct((vec_count, 2 * rank), f32),
             jax.ShapeDtypeStruct((reach, 1, slots), jnp.int32),
-            half_rows,
         ],
         in_specs=[VMEM] * 3 + [any_space],
-        out_specs=[VMEM] * 2 + [any_space] * 2,
-        scratch_shapes=[pltpu.VMEM((rank // 2, 2 * rank), bf16)]
-        + [dma((reach,))] * 2
-        + [dma((count,))] * 2
-        + [dma(())],
+        out_specs=[VMEM] * 2 + [any_space],
+        scratch_shapes=[dma((reach,))] * 2,
         compiler_params=pltpu.CompilerParams(
             collective_id=0, has_side_effects=True, vmem_limit_bytes=LIMIT
         ),
@@ -484,36 +475,36 @@
     near_got = lax.ppermute(spread, "leaf", [(source, source + 1) for source in range(count - 1)])
 
     packed = (reach, cap // 2, vec_count, 2 * rank)
-    coef_got, term_got, roots = pl.pallas_call(
+    coef_got, term_got, others = pl.pallas_call(
         functools.partial(exchange_kernel, count, cap, offsets),
         out_shape=[
             jax.ShapeDtypeStruct(packed, bf16),
             jax.ShapeDtypeStruct(packed, bf16),
-            jax.ShapeDtypeStruct((count, vec_count // 2, 2 * rank), bf16),
+            jax.ShapeDtypeStruct((heights, vec_count, rank), f32),
         ],
-        in_specs=[SMEM] * 3 + [VMEM] * 3,
-        out_specs=[any_space] * 3,
+        in_specs=[SMEM] * 3 + [VMEM] * 3 + [any_space],
+        out_specs=[any_space] * 2 + [VMEM],
         scratch_shapes=[pltpu.VMEM(packed, bf16)] * 2
+        + [pltpu.VMEM((heights - 1, rank, rank), f32)]
+        + [pltpu.VMEM((heights, vec_count, 2 * rank), f32)] * 2
         + [dma((reach,))] * 4
-        + [dma((count,))] * 2
-        + [dma(())],
+        + [dma((heights,))] * 2
+        + [dma((heights - 1,))],
         compiler_params=pltpu.CompilerParams(
             collective_id=1, has_side_effects=True, vmem_limit_bytes=LIMIT
         ),
         name="exchange",
-    )(far_rows, counts, ids, coefs, far_tiles, root)
+    )(far_rows, counts, ids, coefs, far_tiles, root, top_transfer)
 
     chunks = 4
-    top_pairs = top_transfer.reshape(count // 2 - 1, 2 * rank, rank)
     return pl.pallas_call(
         functools.partial(downward_kernel, count, cap, offsets, leaf_count, leaf_size, chunks),
         out_shape=jax.ShapeDtypeStruct((vec_count, points), f32),
-        in_specs=[SMEM] * 4 + [VMEM] * 7 + [any_space] * 5,
+        in_specs=[SMEM] * 4 + [VMEM] * 6 + [any_space] * 5,
         out_specs=any_space,
         scratch_shapes=[
             pltpu.VMEM((nodes, vec_count, rank), f32),
-            pltpu.VMEM((2 * count, vec_count, rank), f32),
-            pltpu.VMEM(top_pairs.shape, f32),
+            pltpu.VMEM(top_transfer.shape, f32),
             pltpu.VMEM(top_couple.shape, f32),
             pltpu.VMEM(leaf_basis.shape, bf16),
             pltpu.VMEM(near_own.shape, f32),
@@ -532,10 +523,9 @@
         far_tiles,
         coef_got,
         term_got,
-        roots,
-        lifts,
+        others,
         local_transfer,
-        top_pairs,
+        top_transfer,
         top_couple,
         leaf_basis,
         near_own,

time: 103 us -> 98.5 us (0.956)
  Pallas kernels: 90.2 us -> 82.1 us
  waiting for transfers between devices: 0.01 us -> 3.83 us
    pallas_call x1, Pallas kernels: 21.3 us -> 8.79 us  [body(): pl.pallas_call(functools.partial(upward_kernel, count, leaf_count, leaf_s...]
    pallas_call x1, Pallas kernels: 40.6 us -> 46.6 us  [body(): pl.pallas_call(functools.partial(exchange_kernel, count, cap, offsets), o...]
    ppermute x1, waiting for transfers between devices: 0.01 us -> 3.83 us  [body(): lax.ppermute(vectors, 'leaf', [(source, source - 1) for source in range(1...]
    pallas_call x1, Pallas kernels: 12.4 us -> 10.9 us  [body(): pl.pallas_call(functools.partial(downward_kernel, count, cap, offsets, le...]
  transfers between devices with their start and end apart: 2 -> 2, of which waited for: 0 -> 1; matrix products, arithmetic and copies ran while one was open for 3% -> 3% of each run, Pallas kernels for 61% -> 57%
where the time goes in v3:
time: 98.5 us; the launch traced here: 96.9 us
  Pallas kernels  82.1 us (83%)
  starting transfers between devices  5.58 us (6%)
  local copies, waits for them, and re-layouts  5.3 us (5%)
  waiting for transfers between devices  3.83 us (4%)
    pallas_call x1, Pallas kernels, body(): pl.pallas_call(functools.partial(exchange_kernel, count, cap, offsets), o...  46.6 us
    pallas_call x1, Pallas kernels, body(): pl.pallas_call(functools.partial(near_kernel, group, steps, leaf_size, po...  15.8 us
    pallas_call x1, Pallas kernels, body(): pl.pallas_call(functools.partial(downward_kernel, count, cap, offsets, le...  10.9 us
    pallas_call x1, Pallas kernels, body(): pl.pallas_call(functools.partial(upward_kernel, count, leaf_count, leaf_s...  8.79 us
    unnamed x7, local copies, waits for them, and re-layouts  5.3 us
    ppermute x1, waiting for transfers between devices, body(): lax.ppermute(vectors, 'leaf', [(source, source - 1) for source in range(1...  3.83 us
    ppermute x1, starting transfers between devices, body(): lax.ppermute(vectors, 'leaf', [(source, source - 1) for source in range(1...  3.67 us
  transfers between devices with their start and end apart: 2, of which 1 were waited for; matrix products, arithmetic and copies ran while one was open for 3% of the time, Pallas kernels for 57%

profile of v3, /device:TPU:8, one launch (start us, length us, event | category | flops | bytes accessed | tf_op | source)
XLA Modules:
  0.0 96.9 jit_solution(12612529730411110011)
XLA Ops:
  0.0 3.7 %collective-permute-start = (bf16[64,8192]{1,0:T(8,128)(2,1)}, bf16[64,8192]{1,0:T(8,128)(2,1)S(1)}, u32[]{:S(2)}, u32[]{:S(2)}) collective-permute-start(bf16[64,8192]{1,0:T(8,128)(2,1)} %vec_ref.3), channel_id=1, source_target_pairs={{1,0},{2,1},{3,2},{4,3},{5,4},{6,5},{7,6},{8,7},{9,8},{10,9},{11,1... | collective-permute-start | bytes 3145736 | tf_op jit(solution)/shard_map/ppermute | solution.py:425
  3.7 8.8 %upward.1 = (bf16[63,64,64]{2,1,0:T(8,128)(2,1)}, f32[64,128]{1,0:T(8,128)}, s32[8,1,144]{2,1,0:T(1,128)}) custom-call(bf16[64,8192]{1,0:T(8,128)(2,1)} %vec_ref.3, bf16[64,8192]{1,0:T(8,128)(2,1)} %basis_hbm.1, bf16[63,64,64]{2,1,0:T(8,128)(2,1)} %transfer_ref.3, s32[1,144]{1,0:T(1,128)} %bitcast.2), custom_call_target="tpu_custom_call" | custom-call | tf_op jit(solution)/shard_map/upward/pallas_call | solution.py:430
  12.5 0.0 copy-start
  12.5 3.8 %collective-permute-done.next_ref = bf16[64,8192]{1,0:T(8,128)(2,1)S(1)} collective-permute-done((bf16[64,8192]{1,0:T(8,128)(2,1)}, bf16[64,8192]{1,0:T(8,128)(2,1)S(1)}, u32[]{:S(2)}, u32[]{:S(2)}) %collective-permute-start) | collective-permute-done | bytes 1048608 | tf_op jit(solution)/shard_map/ppermute | solution.py:425
  16.3 0.0 copy-start.2
  16.3 1.0 copy-done.2
  17.3 15.8 %near.1 = (f32[64,8192]{1,0:T(8,128)}, bf16[64,8192]{1,0:T(8,128)(2,1)}) custom-call(s32[96]{0:T(128)} %rows_ref.3, s32[96]{0:T(128)} %cols_ref.2, bf16[64,8192]{1,0:T(8,128)(2,1)} %vec_ref.3, bf16[64,8192]{1,0:T(8,128)(2,1)} %copy-done.2, bf16[96,256,256]{2,1,0:T(8,128)(2,1)} %tiles_ref.3), custom_call_target="tpu_custom_call" | custom-call | tf_op jit(solution)/shard_map/near/pallas_call | solution.py:448
  33.1 1.9 %collective-permute-start.1 = (bf16[64,8192]{1,0:T(8,128)(2,1)}, bf16[64,8192]{1,0:T(8,128)(2,1)S(1)}, u32[]{:S(2)}, u32[]{:S(2)}) collective-permute-start(bf16[64,8192]{1,0:T(8,128)(2,1)} %get-tuple-element.24), channel_id=1, source_target_pairs={{0,1},{1,2},{2,3},{3,4},{4,5},{5,6},{6,7},{7,8},{8,9},{9,10},{10,1... | collective-permute-start | bytes 3145736 | tf_op jit(solution)/shard_map/ppermute | solution.py:475
  35.0 0.0 copy-done
  35.0 3.4 %copy.14.tiles_ref = bf16[144,64,64]{2,1,0:T(8,128)(2,1)} copy(bf16[144,64,64]{0,2,1:T(8,128)(2,1)S(1)} %copy-done) | data formatting | bytes 2359296 | tf_op args[6]
  38.4 46.6 %exchange.1 = (bf16[8,8,64,128]{3,2,1,0:T(8,128)(2,1)}, bf16[8,8,64,128]{3,2,1,0:T(8,128)(2,1)}, f32[5,64,64]{2,1,0:T(8,128)}) custom-call(s32[144]{0:T(256)} %rows_ref.5, s32[9]{0:T(128)} %bitcast.3, s32[8,1,144]{2,1,0:T(1,128)} %get-tuple-element.15.ids_ref, bf16[63,64,64]{2,1,0:T(8,128)(2,1)} %get-tuple-element.18.coef_ref, ...), custom_call_target="tpu_custom_call" | custom-call | tf_op jit(solution)/shard_map/exchange/pallas_call | solution.py:478
  85.0 0.0 collective-permute-done.1.got_hbm
  85.0 0.0 copy-start.1
  85.0 1.0 copy-done.1
  86.0 10.9 %downward.1 = f32[64,8192]{1,0:T(8,128)} custom-call(s32[144]{0:T(256)} %rows_ref.5, s32[144]{0:T(256)} %cols_ref.3, s32[9]{0:T(128)} %bitcast.4, s32[8,1,144]{2,1,0:T(1,128)} %get-tuple-element.15.ids_ref, bf16[63,64,64]{2,1,0:T(8,128)(2,1)} %get-tuple-element.18.coef_ref, bf16[144,64,64]{2,1,0:T(8,128)(2,1)} %copy.14.tiles_ref, ...), custom_call_target="tpu_custom_call" | custom-call | tf_op jit(solution)/shard_map/downward/pallas_call | solution.py:500
Async XLA Ops:
  0.0 16.3 %collective-permute-start = (bf16[64,8192]{1,0:T(8,128)(2,1)}, bf16[64,8192]{1,0:T(8,128)(2,1)S(1)}, u32[]{:S(2)}, u32[]{:S(2)}) collective-permute-start(bf16[64,8192]{1,0:T(8,128)(2,1)} %vec_ref.3), channel_id=1, source_target_pairs={{1,0},{2,1},{3,2},{4,3},{5,4},{6,5},{7,6},{8,7},{9,8},{10,9},{11,1... | collective-permute-start | bytes 3145736 | tf_op jit(solution)/shard_map/ppermute | solution.py:425
  12.5 22.5 %copy-start = (bf16[144,64,64]{0,2,1:T(8,128)(2,1)S(1)}, bf16[144,64,64]{0,2,1:T(8,128)(2,1)}, u32[]{:S(2)}) copy-start(bf16[144,64,64]{0,2,1:T(8,128)(2,1)} %param.18) | copy-start | bytes 3538948
  16.3 1.0 %copy-start.2 = (bf16[64,8192]{1,0:T(8,128)(2,1)}, bf16[64,8192]{1,0:T(8,128)(2,1)S(1)}, u32[]{:S(2)}) copy-start(bf16[64,8192]{1,0:T(8,128)(2,1)S(1)} %collective-permute-done.next_ref) | copy-start | bytes 3145732
  33.1 51.9 %collective-permute-start.1 = (bf16[64,8192]{1,0:T(8,128)(2,1)}, bf16[64,8192]{1,0:T(8,128)(2,1)S(1)}, u32[]{:S(2)}, u32[]{:S(2)}) collective-permute-start(bf16[64,8192]{1,0:T(8,128)(2,1)} %get-tuple-element.24), channel_id=1, source_target_pairs={{0,1},{1,2},{2,3},{3,4},{4,5},{5,6},{6,7},{7,8},{8,9},{9,10},{10,1... | collective-permute-start | bytes 3145736 | tf_op jit(solution)/shard_map/ppermute | solution.py:475
  85.0 1.0 %copy-start.1 = (bf16[64,8192]{1,0:T(8,128)(2,1)}, bf16[64,8192]{1,0:T(8,128)(2,1)S(1)}, u32[]{:S(2)}) copy-start(bf16[64,8192]{1,0:T(8,128)(2,1)S(1)} %collective-permute-done.1.got_hbm) | copy-start | bytes 3145732
